TPU v7x, 32 devices: a whole 2x2x4 slice. The times are simulated.
32 devices in a mesh: grp: 2 (over x), ch: 4 (over y, core), sp: 4 (over z).
Axes of the slice: x: 2, y: 2, z: 4, core: 2. Of those that a mesh axis runs over, the one named last changes fastest.
Arguments:
- features: bfloat16 [1024, 64, 128], P(('grp', 'ch'), 'sp'), parts along dimension 0, may hold values from -6 to 6
- saved_mix: bfloat16 [1024, 64, 128], P(('grp', 'ch'), 'sp'), parts along dimension 0, may hold values from -6 to 6
- out_grad: bfloat16 [1024, 64, 128], P(('grp', 'ch'), 'sp'), parts along dimension 0, may hold values from -6 to 6
- kernel: bfloat16 [512, 31, 31], P('ch'), may hold values from -0.1875 to 0.1875
- w_in: bfloat16 [512, 2048], P(None, 'ch'), may hold values from -0.25 to 0.25
- w_out: bfloat16 [2048, 512], P('ch'), may hold values from -0.125 to 0.125
Outputs:
- in_grad: float32 [1024, 64, 128], P(('grp', 'ch'), 'sp'), parts along dimension 0
- kernel_grad: float32 [1024, 31, 31], P(('grp', 'ch')), parts along dimension 0
- w_in_grad: float32 [1024, 2048], P('grp', ('ch', 'sp')), parts along dimension 0
- w_out_grad: float32 [4096, 512], P(('grp', 'ch', 'sp')), parts along dimension 0
There are 2 independent parts, one for each index of `grp`. A program takes and returns all parts, laid end to end along the dimension named above; an argument that names none is the same for every part. Nothing has to cross between parts.
All inputs are finite; a program needn't handle non-finite values.
Results may differ from a plain program's by a relative error of at most 0.0041.
Values may be sent and summed in bfloat16 or wider, within the bound.
A program may use at most 64 MiB of HBM per device.

v0:
```python
import math

import jax
import jax.numpy as jnp
from jax import lax
from jax.sharding import PartitionSpec as P

SQRT_HALF = 0.7071067811865476
INV_ROOT_TAU = 0.3989422804014327


def with_halo(block, sides, width):
    for axis, dim in sides:
        count = lax.axis_size(axis)
        forward = [(i, i + 1) for i in range(count - 1)]
        backward = [(target, source) for source, target in forward]
        low = lax.ppermute(
            lax.slice_in_dim(block, block.shape[dim] - width, None, axis=dim), axis, forward
        )
        high = lax.ppermute(lax.slice_in_dim(block, 0, width, axis=dim), axis, backward)
        block = jnp.concatenate([low, block, high], axis=dim)
    return block


def depthwise(source, taps):
    return lax.conv_general_dilated(
        source[None],
        taps[:, None],
        (1, 1),
        "VALID",
        dimension_numbers=("NCHW", "OIHW", "NCHW"),
        feature_group_count=source.shape[0],
        preferred_element_type=jnp.float32,
    )[0]


def contract_last(left, right):
    return lax.dot_general(
        left, right, (((1,), (1,)), ((), ())), preferred_element_type=jnp.float32
    )


def contract_first(left, right):
    return lax.dot_general(
        left, right, (((0,), (0,)), ((), ())), preferred_element_type=jnp.float32
    )


def pointwise_back(mixed_rows, grad_rows, w_in_block, w_out_block):
    preact = contract_first(w_in_block, mixed_rows)
    normal_cdf = 0.5 * (1.0 + jax.scipy.special.erf(preact * SQRT_HALF))
    normal_pdf = INV_ROOT_TAU * jnp.exp(-0.5 * preact * preact)
    hidden = (preact * normal_cdf).astype(jnp.bfloat16)
    hidden_grad = jnp.dot(w_out_block, grad_rows, preferred_element_type=jnp.float32)
    preact_grad = (hidden_grad * (normal_cdf + preact * normal_pdf)).astype(jnp.bfloat16)
    return (hidden, preact_grad)


def per_device(features, saved_mix, out_grad, kernel, w_in, w_out):
    local_ch, rows, width = features.shape
    local_pos = rows * width
    half = kernel.shape[1] // 2
    factor = 1.0 / math.sqrt(local_pos * lax.axis_size("sp"))
    mixed_rows = saved_mix.reshape(local_ch, local_pos)
    grad_rows = out_grad.reshape(local_ch, local_pos)
    mixed_all, grad_all = (
        lax.all_gather(mixed_rows, "ch", axis=0, tiled=True),
        lax.all_gather(grad_rows, "ch", axis=0, tiled=True),
    )
    hidden, preact_grad = pointwise_back(mixed_all, grad_all, w_in, w_out)
    w_in_local = contract_last(mixed_all, preact_grad)
    w_out_local = contract_last(grad_all, hidden)
    mix_grad = lax.psum_scatter(
        jnp.dot(w_in, preact_grad, preferred_element_type=jnp.float32),
        "ch",
        scatter_dimension=0,
        tiled=True,
    ).astype(jnp.bfloat16)
    w_in_sum, w_out_sum = (
        lax.psum_scatter(w_in_local, "sp", scatter_dimension=1, tiled=True),
        lax.psum_scatter(w_out_local, "sp", scatter_dimension=1, tiled=True),
    )
    mix_grad = mix_grad.reshape(local_ch, rows, width)
    rimmed = with_halo(mix_grad, (("sp", 1),), half)
    padded = jnp.pad(rimmed, ((0, 0), (0, 0), (half, half)))
    in_grad = out_grad.astype(jnp.float32) + depthwise(padded, kernel[:, ::-1, ::-1])
    kernel_part = depthwise(padded, features)
    kernel_grad = lax.psum(kernel_part, "sp")[:, ::-1, ::-1] * factor
    return (in_grad, kernel_grad, w_in_sum * factor, w_out_sum.T * factor)


def solution(mesh):
    return jax.shard_map(
        per_device,
        mesh=mesh,
        in_specs=(
            P(("grp", "ch"), "sp", None),
            P(("grp", "ch"), "sp", None),
            P(("grp", "ch"), "sp", None),
            P("ch", None, None),
            P(None, "ch"),
            P("ch", None),
        ),
        out_specs=(
            P(("grp", "ch"), "sp", None),
            P(("grp", "ch"), None, None),
            P("grp", ("ch", "sp")),
            P(("grp", "ch", "sp"), None),
        ),
        check_vma=False,
    )
```

profile of v0, /device:TPU:0, one launch (start us, length us, event | category | flops | bytes accessed | tf_op | source)
XLA Modules:
  0.0 533.9 jit_solution(92826388484412066)
XLA Ops:
  7.2 2.0 copy.34
  9.3 2.0 copy.35
  11.4 24.1 %all-gather.5.cloned.1.call-done = bf16[512,2048]{1,0:T(8,128)(2,1)} async-done(((bf16[128,2048]{1,0:T(8,128)(2,1)}), bf16[512,2048]{1,0:T(8,128)(2,1)}) %all-gather.5.cloned.1.call-update) | async-done | bytes 2097168 | tf_op jit(solution)/shard_map/all_gather | solution.py:67
  35.5 4.8 fusion.21
  40.3 19.3 %all-gather.3.cloned.1.call-done = bf16[512,2048]{1,0:T(8,128)(2,1)} async-done(((bf16[128,2048]{1,0:T(8,128)(2,1)}), bf16[512,2048]{1,0:T(8,128)(2,1)}) %all-gather.3.cloned.1.call-update) | async-done | bytes 2097168 | tf_op jit(solution)/shard_map/all_gather | solution.py:68
  59.7 4.6 fusion.5
  64.3 3.3 convolution_bitcast_fusion
  67.6 3.9 convolution_bitcast_fusion.1
  71.6 5.8 %fusion.18 = f32[512,512]{0,1:T(8,128)} fusion(bf16[512,2048]{1,0:T(8,128)(2,1)} %all-gather.3.cloned.1.call-done, f32[512,2048]{1,0:T(8,128)} %fusion.21), kind=kOutput, calls=%fused_computation.24 | convolution fusion | flops 1078984704 | bytes 7340032 | tf_op jit(solution)/shard_map/dot_general | solution.py:38
  77.5 34.7 %reduce-scatter.4.cloned.1.call-done = f32[128,2048]{0,1:T(8,128)} async-done(((f32[512,2048]{0,1:T(8,128)}), f32[128,2048]{0,1:T(8,128)}) %reduce-scatter.4.cloned.1.call-update) | async-done | bytes 1048592 | tf_op jit(solution)/shard_map/reduce_scatter | solution.py:73
  112.2 1.3 convert_element_type.16
  113.5 1.0 fusion.20
  114.5 3.4 collective-permute-start
  117.9 1.5 collective-permute-start.1
  119.4 1.2 copy.15
  121.5 1.5 copy.19
  123.0 28.5 %reduce-scatter.6.cloned.1.call-done = f32[512,128]{0,1:T(8,128)} async-done(((f32[512,512]{0,1:T(8,128)}), f32[512,128]{0,1:T(8,128)}) %reduce-scatter.6.cloned.1.call-update) | async-done | bytes 262160 | tf_op jit(solution)/shard_map/reduce_scatter | solution.py:80
  153.3 25.4 %reduce-scatter.8.cloned.1.call-done = f32[512,128]{0,1:T(8,128)} async-done(((f32[512,512]{0,1:T(8,128)}), f32[512,128]{0,1:T(8,128)}) %reduce-scatter.8.cloned.1.call-update) | async-done | bytes 262160 | tf_op jit(solution)/shard_map/reduce_scatter | solution.py:81
  178.7 1.8 multiply_bitcast_fusion
  181.2 1.8 fusion.17
  183.0 173.5 %fusion.7 = f32[1,128,31,31]{1,0,3,2:T(1,128)S(1)} fusion(bf16[128,1,16,128]{0,1,3,2:T(2,128)(2,1)S(1)} %copy-done.3, bf16[1,128,46,158]{1,3,2,0:T(8,128)(2,1)S(1)} %fusion.17), kind=kOutput, calls=%fused_computation.13 | convolution fusion | flops 503840768 | bytes 2876928 | tf_op jit(solution)/shard_map/conv_general_dilated | solution.py:26
  357.6 166.1 %fusion.9 = f32[1,128,16,128]{1,0,3,2:T(1,128)S(1)} fusion(bf16[1,128,46,158]{1,3,2,0:T(8,128)(2,1)S(1)} %fusion.17, bf16[128,1,31,31]{0,3,2,1:T(8,128)(2,1)} %bitcast.44), kind=kOutput, calls=%fused_computation.15 | convolution fusion | flops 503840768 | bytes 3155200 | tf_op jit(solution)/shard_map/conv_general_dilated | solution.py:26
  523.8 1.4 copy.20
  525.2 1.9 broadcast_multiply_fusion
  (37 shorter events, 4.9 us)
Async XLA Ops:
  7.2 28.3 %copy-start = (bf16[512,512]{1,0:T(8,128)(2,1)S(1)}, bf16[512,512]{1,0:T(8,128)(2,1)}, u32[]{:S(2)}) copy-start(bf16[512,512]{1,0:T(8,128)(2,1)} %param.10) | copy-start | bytes 1572868
  7.2 28.3 %all-gather.5.cloned.1.call-start = ((), (), s32[]{:S(2)}) async-start(), calls=%async_computation.4 | async-start | bytes 2621440 | tf_op jit(solution)/shard_map/all_gather | solution.py:67
  9.3 50.4 %all-gather.3.cloned.1.call-start = ((), (), s32[]{:S(2)}) async-start(), calls=%async_computation.3 | async-start | bytes 2621440 | tf_op jit(solution)/shard_map/all_gather | solution.py:68
  11.3 48.4 %copy-start.7 = (bf16[512,512]{1,0:T(8,128)(2,1)S(1)}, bf16[512,512]{1,0:T(8,128)(2,1)}, u32[]{:S(2)}) copy-start(bf16[512,512]{1,0:T(8,128)(2,1)} %param.11) | copy-start | bytes 1572868
  11.3 100.9 %reduce-scatter.4.cloned.1.call-start = ((), (), s32[]{:S(2)}) async-start(), calls=%async_computation.5 | async-start | bytes 5242880 | tf_op jit(solution)/shard_map/reduce_scatter | solution.py:73
  67.6 83.9 %reduce-scatter.6.cloned.1.call-start = ((), (), s32[]{:S(2)}) async-start(), calls=%async_computation.7 | async-start | bytes 1310720 | tf_op jit(solution)/shard_map/reduce_scatter | solution.py:80
  71.6 107.1 %reduce-scatter.8.cloned.1.call-start = ((), (), s32[]{:S(2)}) async-start(), calls=%async_computation.8 | async-start | bytes 1310720 | tf_op jit(solution)/shard_map/reduce_scatter | solution.py:81
  77.4 42.0 %copy-start.2 = (bf16[128,16,128]{2,1,0:T(8,128)(2,1)S(1)}, bf16[128,16,128]{2,1,0:T(8,128)(2,1)}, u32[]{:S(2)}) copy-start(bf16[128,16,128]{2,1,0:T(8,128)(2,1)} %param.8) | copy-start | bytes 1572868
  77.4 43.2 %copy-start.6 = (bf16[128,31,31]{0,2,1:T(8,128)(2,1)S(1)}, bf16[128,31,31]{0,2,1:T(8,128)(2,1)}, u32[]{:S(2)}) copy-start(bf16[128,31,31]{0,2,1:T(8,128)(2,1)} %param.9) | copy-start | bytes 738052
  77.4 44.1 %copy-start.4 = (bf16[128,16,128]{2,1,0:T(8,128)(2,1)S(1)}, bf16[128,16,128]{2,1,0:T(8,128)(2,1)}, u32[]{:S(2)}) copy-start(bf16[128,16,128]{2,1,0:T(8,128)(2,1)} %param.6) | copy-start | bytes 1572868
  77.5 447.7 %all-reduce.3.cloned.1.call-start = ((), (), s32[]{:S(2)}) async-start(), calls=%async_computation.6 | async-start | bytes 1015808 | tf_op jit(solution)/shard_map/psum | solution.py:88
  114.5 65.9 %collective-permute-start = (bf16[128,15,128]{0,2,1:T(8,128)(2,1)}, bf16[128,15,128]{0,2,1:T(8,128)(2,1)S(1)}, u32[]{:S(2)}, u32[]{:S(2)}) collective-permute-start(bf16[128,15,128]{0,2,1:T(8,128)(2,1)} %get-tuple-element.12), channel_id=1, source_target_pairs={{0,1},{1,2},{2,3},{4,5},{5,6},{6,7},{8,9},{9,10},{10,11},{12,13},{... | collective-permute-start | bytes 1474568 | tf_op jit(solution)/shard_map/ppermute | solution.py:17
  117.9 63.3 %collective-permute-start.1 = (bf16[128,15,128]{0,2,1:T(8,128)(2,1)S(1)}, bf16[128,15,128]{0,2,1:T(8,128)(2,1)}, u32[]{:S(2)}, u32[]{:S(2)}) collective-permute-start(bf16[128,15,128]{0,2,1:T(8,128)(2,1)S(1)} %get-tuple-element.13), channel_id=1, source_target_pairs={{1,0},{2,1},{3,2},{5,4},{6,5},{7,6},{9,8},{10,9},{11,10},{13,12},{... | collective-permute-start | bytes 1474568 | tf_op jit(solution)/shard_map/ppermute | solution.py:20
  178.7 4.3 copy-start.3
  180.4 0.8 copy-start.5
  357.5 166.1 %copy-start.1 = (bf16[128,16,128]{0,2,1:T(8,128)(2,1)S(1)}, bf16[128,16,128]{0,2,1:T(8,128)(2,1)}, u32[]{:S(2)}) copy-start(bf16[128,16,128]{0,2,1:T(8,128)(2,1)} %copy.15) | copy-start | bytes 1572868
Sparse Core Ops, SparseCore 0:
  10.1 25.2 all-gather.4
  37.0 22.5 all-gather.2
  67.7 44.4 reduce-scatter.3
  114.5 36.9 reduce-scatter.5
  153.6 25.0 reduce-scatter.7
  357.7 36.7 all-reduce.2
where the time goes:
time: 534 us
  matrix products  362 us (68%)
  waiting for transfers between devices  132 us (25%)
  between operations  14.2 us (3%)
  local copies, waits for them, and re-layouts  12.6 us (2%)
  other arithmetic  7.77 us (1%)
    conv_general_dilated x2, matrix products, depthwise(): lax.conv_general_dilated(source[None], taps[:, None], (1, 1), 'VALID', di...  340 us
    reduce_scatter x1, waiting for transfers between devices, per_device(): lax.psum_scatter(jnp.dot(w_in, preact_grad, preferred_element_type=jnp.fl...  34.7 us
    reduce_scatter x1, waiting for transfers between devices, per_device(): lax.psum_scatter(w_in_local, 'sp', scatter_dimension=1, tiled=True)  28.5 us
    reduce_scatter x1, waiting for transfers between devices, per_device(): lax.psum_scatter(w_out_local, 'sp', scatter_dimension=1, tiled=True)  25.4 us
    all_gather x1, waiting for transfers between devices, per_device(): lax.all_gather(mixed_rows, 'ch', axis=0, tiled=True)  24.1 us
    all_gather x1, waiting for transfers between devices, per_device(): lax.all_gather(grad_rows, 'ch', axis=0, tiled=True)  19.3 us
  transfers between devices with their start and end apart: 8, of which 5 were waited for; matrix products, arithmetic and copies ran while one was open for 36% of the time, Pallas kernels for 0%

commit v1 on v0

v1 whole, which is shorter than its diff:
```python
import functools
import math

import jax
import jax.numpy as jnp
from jax import lax
from jax.experimental import pallas as pl
from jax.experimental.pallas import tpu as pltpu
from jax.sharding import PartitionSpec as P

SQRT_HALF = 0.7071067811865476
INV_ROOT_TAU = 0.3989422804014327
GROUP = 8


def up(count, unit):
    return -(-count // unit) * unit


def conv_kernel(size, rim_ref, feat_ref, grad_ref, base_ref, in_ref, part_ref):
    group, depth, width = rim_ref.shape
    rows = feat_ref.shape[1]
    half = size // 2
    total = base_ref.shape[1]
    lane = lax.broadcasted_iota(jnp.int32, (depth, width), 1)
    for c in range(group):
        rim = rim_ref[c]
        pieces = []
        for b in range(size):
            shift = b - half
            if shift == 0:
                pieces.append(rim)
                continue
            moved = pltpu.roll(rim, (-shift) % width, 1)
            inside = (lane < width - shift) if shift > 0 else (lane >= -shift)
            pieces.append(jnp.where(inside, moved, jnp.zeros_like(moved)))
        pieces.append(jnp.zeros((total - size * depth, width), rim.dtype))
        stacked = jnp.concatenate(pieces, axis=0)
        line = jnp.broadcast_to(base_ref[c : c + 1, :], (rows, total))
        band = pltpu.roll(line, 0, 1, stride=1, stride_axis=0).astype(jnp.bfloat16)
        in_ref[c] = grad_ref[c].astype(jnp.float32) + jnp.dot(
            band, stacked, preferred_element_type=jnp.float32
        )
        cross = lax.dot_general(
            feat_ref[c], stacked, (((1,), (1,)), ((), ())), preferred_element_type=jnp.float32
        )
        aligned = pltpu.roll(cross, total - (rows - 1), 1, stride=1, stride_axis=0)
        part_ref[c : c + 1, :] = jnp.sum(aligned, axis=0, keepdims=True)


def conv_back(rim, feat_reversed, grad, base, size):
    channels, depth, width = rim.shape
    rows = feat_reversed.shape[1]
    total = base.shape[1]
    group = math.gcd(channels, GROUP)
    block = lambda *dims: pl.BlockSpec((group,) + dims, lambda i: (i,) + (0,) * len(dims))
    return pl.pallas_call(
        functools.partial(conv_kernel, size),
        grid=(channels // group,),
        out_shape=(
            jax.ShapeDtypeStruct((channels, rows, width), jnp.float32),
            jax.ShapeDtypeStruct((channels, total), jnp.float32),
        ),
        in_specs=[block(depth, width), block(rows, width), block(rows, width), block(total)],
        out_specs=(block(rows, width), block(total)),
        compiler_params=pltpu.CompilerParams(vmem_limit_bytes=24 * 1024 * 1024),
        cost_estimate=pl.CostEstimate(
            flops=channels * rows * width * total * 4 * 8,
            bytes_accessed=channels * width * (depth * 2 + rows * 8) + channels * total * 8,
            transcendentals=0,
        ),
    )(rim, feat_reversed, grad, base)


def contract_last(left, right):
    return lax.dot_general(
        left, right, (((1,), (1,)), ((), ())), preferred_element_type=jnp.float32
    )


def contract_first(left, right):
    return lax.dot_general(
        left, right, (((0,), (0,)), ((), ())), preferred_element_type=jnp.float32
    )


def matmul(left, right):
    return jnp.dot(left, right, preferred_element_type=jnp.float32)


def pointwise_back(mixed_rows, grad_rows, w_in_block, w_out_block):
    preact = contract_first(w_in_block, mixed_rows)
    normal_cdf = 0.5 * (1.0 + jax.scipy.special.erf(preact * SQRT_HALF))
    normal_pdf = INV_ROOT_TAU * jnp.exp(-0.5 * preact * preact)
    hidden = (preact * normal_cdf).astype(jnp.bfloat16)
    hidden_grad = matmul(w_out_block, grad_rows)
    preact_grad = (hidden_grad * (normal_cdf + preact * normal_pdf)).astype(jnp.bfloat16)
    return (hidden, preact_grad)


def per_device(features, saved_mix, out_grad, kernel, w_in, w_out):
    local_ch, rows, width = features.shape
    size = kernel.shape[1]
    half = size // 2
    local_pos = rows * width
    count = lax.axis_size("ch")
    chips = count // 2
    me = lax.axis_index("ch")
    factor = 1.0 / math.sqrt(local_pos * lax.axis_size("sp"))

    flip = [(i, i ^ 1) for i in range(count)]
    across = lambda step: [(i, (i + 2 * step) % count) for i in range(count)]
    swap = lambda value: lax.ppermute(value, "ch", flip)
    owner = [
        lax.rem(me // 2 + step, chips) * 2 + (me % 2 if core == 0 else 1 - me % 2)
        for step in range(chips)
        for core in range(2)
    ]

    def gathered(block):
        held = []
        for step in range(chips):
            mine = block if step == 0 else lax.ppermute(block, "ch", across(chips - step))
            held += [mine, swap(mine)]
        return jnp.concatenate(held, axis=0)

    w_in_own = jnp.concatenate(
        [lax.dynamic_slice_in_dim(w_in, at * local_ch, local_ch, 0) for at in owner], axis=0
    )
    w_out_own = jnp.concatenate(
        [lax.dynamic_slice_in_dim(w_out, at * local_ch, local_ch, 1) for at in owner], axis=1
    )
    mixed_all = gathered(saved_mix.reshape(local_ch, local_pos))
    grad_all = gathered(out_grad.reshape(local_ch, local_pos))
    hidden, preact_grad = pointwise_back(mixed_all, grad_all, w_in_own, w_out_own)

    part = lambda index: matmul(
        w_in_own[index * local_ch : (index + 1) * local_ch], preact_grad
    )
    pair = [None] * chips
    for step in list(range(1, chips)) + [0]:
        away = swap(part(2 * step + 1).astype(jnp.bfloat16))
        pair[step] = part(2 * step) + away.astype(jnp.float32)
    pieces = 2 if local_ch % 32 == 0 else 1
    chunk = local_ch // pieces

    depth = up(rows + size - 1, 16)
    total = up(size * depth, 128)
    flipped = kernel[:, ::-1, ::-1].astype(jnp.float32).transpose(0, 2, 1)
    base = jnp.pad(flipped, ((0, 0), (0, 0), (0, depth - size))).reshape(local_ch, size * depth)
    base = jnp.pad(base, ((0, 0), (0, total - size * depth)))
    feat_reversed = features[:, ::-1]
    hops = lax.axis_size("sp")
    forward = [(i, i + 1) for i in range(hops - 1)]
    backward = [(i + 1, i) for i in range(hops - 1)]

    in_grads, kernel_grads = [], []
    for piece in range(pieces):
        at = slice(piece * chunk, (piece + 1) * chunk)
        mix = pair[0][at]
        for step in range(1, chips):
            sent = pair[step][at].astype(jnp.bfloat16)
            mix = mix + lax.ppermute(sent, "ch", across(step)).astype(jnp.float32)
        mix = mix.astype(jnp.bfloat16).reshape(chunk, rows, width)
        low, high, left = [], [], half
        below, above = mix, mix
        while left > 0:
            take = min(left, rows)
            below = lax.ppermute(below[:, rows - take :] if below.shape[1] >= take else below, "sp", forward)
            above = lax.ppermute(above[:, :take], "sp", backward)
            low.insert(0, below)
            high.append(above)
            left -= take
        rim = jnp.concatenate(
            low + [mix] + high + [jnp.zeros((chunk, depth - rows - size + 1, width), mix.dtype)],
            axis=1,
        )
        in_part, kernel_part = conv_back(
            rim, feat_reversed[at], out_grad[at], base[at], size
        )
        in_grads.append(in_part)
        kernel_part = kernel_part[:, : size * depth].reshape(chunk, size, depth)[:, :, :size]
        kernel_grads.append(lax.psum(kernel_part, "sp"))

    def absolute(value):
        blocks = []
        for j in range(count):
            step = lax.rem(j // 2 - me // 2 + chips, chips)
            place = step * 2 + lax.rem(me + j, 2)
            blocks.append(lax.dynamic_slice_in_dim(value, place * local_ch, local_ch, 0))
        return jnp.concatenate(blocks, axis=0)

    w_in_sum = lax.psum_scatter(
        absolute(contract_last(mixed_all, preact_grad)), "sp", scatter_dimension=1, tiled=True
    )
    w_out_sum = lax.psum_scatter(
        absolute(contract_last(grad_all, hidden)), "sp", scatter_dimension=1, tiled=True
    )
    in_grad = jnp.concatenate(in_grads, axis=0)
    kernel_grad = jnp.concatenate(kernel_grads, axis=0).transpose(0, 2, 1)[:, ::-1, ::-1] * factor
    return (in_grad, kernel_grad, w_in_sum * factor, w_out_sum.T * factor)


def solution(mesh):
    return jax.shard_map(
        per_device,
        mesh=mesh,
        in_specs=(
            P(("grp", "ch"), "sp", None),
            P(("grp", "ch"), "sp", None),
            P(("grp", "ch"), "sp", None),
            P("ch", None, None),
            P(None, "ch"),
            P("ch", None),
        ),
        out_specs=(
            P(("grp", "ch"), "sp", None),
            P(("grp", "ch"), None, None),
            P("grp", ("ch", "sp")),
            P(("grp", "ch", "sp"), None),
        ),
        check_vma=False,
    )
```

time: 534 us -> 266 us (0.50)
  matrix products: 362 us -> 13.9 us
  waiting for transfers between devices: 132 us -> 161 us
  Pallas kernels: 0 us -> 27.4 us
  starting transfers between devices: 5.13 us -> 18.3 us
  local copies, waits for them, and re-layouts: 12.6 us -> 23.9 us
    conv_general_dilated x2 -> x0, matrix products: 340 us -> none  [depthwise(): lax.conv_general_dilated(source[None], taps[:, None], (1, 1), 'VALID', di...]
    psum x1, waiting for transfers between devices: 0.01 us -> 82.5 us  [per_device(): kernel_grads.append(lax.psum(kernel_part, 'sp'))]
    all_gather x2 -> x0, waiting for transfers between devices: 43.4 us -> none  [the longest x1 24.1 us: per_device(): lax.all_gather(mixed_rows, 'ch', axis=0, tiled=True)]
    reduce_scatter x3 -> x2, waiting for transfers between devices: 88.6 us -> 50.8 us  [the longest x1 26.3 us: per_device(): lax.psum_scatter(absolute(contract_last(mixed_all, preact_grad)), 'sp', s...]
    ppermute x2 -> x14, waiting for transfers between devices: 0.01 us -> 27.5 us  [the longest x2 12.7 us: gathered(): lax.ppermute(block, 'ch', across(chips - step))]
    pallas_call x0 -> x2, Pallas kernels: none -> 27.4 us  [conv_back(): pl.pallas_call(functools.partial(conv_kernel, size), grid=(channels // gr...]
    ppermute x2 -> x14, starting transfers between devices: 4.88 us -> 18.1 us  [the longest x2 9.3 us: per_device(): lax.ppermute(below[:, rows - take:] if below.shape[1] >= take else below,...]
    unnamed x22 -> x31, local copies, waits for them, and re-layouts: 8.31 us -> 14.9 us
  transfers between devices with their start and end apart: 8 -> 17, of which waited for: 5 -> 10; matrix products, arithmetic and copies ran while one was open for 36% -> 12% of each run, Pallas kernels for 0% -> 0%
where the time goes in v1:
time: 266 us
  waiting for transfers between devices  161 us (61%)
  Pallas kernels  27.4 us (10%)
  local copies, waits for them, and re-layouts  23.9 us (9%)
  starting transfers between devices  18.3 us (7%)
  between operations  14.2 us (5%)
  matrix products  13.9 us (5%)
  other arithmetic  6.99 us (3%)
    psum x1, waiting for transfers between devices, per_device(): kernel_grads.append(lax.psum(kernel_part, 'sp'))  82.5 us
    pallas_call x2, Pallas kernels, conv_back(): pl.pallas_call(functools.partial(conv_kernel, size), grid=(channels // gr...  27.4 us
    reduce_scatter x1, waiting for transfers between devices, per_device(): lax.psum_scatter(absolute(contract_last(mixed_all, preact_grad)), 'sp', s...  26.3 us
    reduce_scatter x1, waiting for transfers between devices, per_device(): lax.psum_scatter(absolute(contract_last(grad_all, hidden)), 'sp', scatter...  24.5 us
    unnamed x31, local copies, waits for them, and re-layouts  14.9 us
    ppermute x2, waiting for transfers between devices, gathered(): lax.ppermute(block, 'ch', across(chips - step))  12.7 us
    ppermute x2, waiting for transfers between devices, per_device(): mix = mix + lax.ppermute(sent, 'ch', across(step)).astype(jnp.float32)  11.7 us
    ppermute x2, starting transfers between devices, per_device(): lax.ppermute(below[:, rows - take:] if below.shape[1] >= take else below,...  9.3 us
  transfers between devices with their start and end apart: 17, of which 10 were waited for; matrix products, arithmetic and copies ran while one was open for 12% of the time, Pallas kernels for 0%

profile of v1, /device:TPU:0, one launch (start us, length us, event | category | flops | bytes accessed | tf_op | source)
XLA Modules:
  0.0 265.5 jit_solution(1431323315394572705)
XLA Ops:
  7.2 2.0 copy.34
  9.7 2.5 collective-permute-start.4
  12.2 2.0 copy.35
  19.9 5.4 %collective-permute-done.4 = bf16[128,2048]{1,0:T(8,128)(2,1)} collective-permute-done((bf16[128,2048]{1,0:T(8,128)(2,1)}, bf16[128,2048]{1,0:T(8,128)(2,1)}, u32[]{:S(2)}, u32[]{:S(2)}) %collective-permute-start.4) | collective-permute-done | bytes 524320 | tf_op jit(solution)/shard_map/ppermute | solution.py:123
  25.3 1.9 constant_dynamic-update-slice_fusion.6
  27.2 1.9 constant_dynamic-update-slice_fusion.5
  29.1 7.3 %collective-permute-done.1 = bf16[128,2048]{1,0:T(8,128)(2,1)} collective-permute-done((bf16[128,2048]{1,0:T(8,128)(2,1)}, bf16[128,2048]{1,0:T(8,128)(2,1)}, u32[]{:S(2)}, u32[]{:S(2)}) %collective-permute-start.1) | collective-permute-done | bytes 524320 | tf_op jit(solution)/shard_map/ppermute | solution.py:123
  39.4 2.9 %fusion.16 = f32[512,2048]{1,0:T(8,128)S(1)} fusion(bf16[512,2048]{1,0:T(8,128)(2,1)} %constant_dynamic-update-slice_fusion.4, bf16[128,512]{1,0:T(8,128)(2,1)S(1)} %get-tuple-element.50, bf16[128,512]{1,0:T(8,128)(2,1)S(1)} %get-tuple-element.51, bf16[128,512]{1,0:T(8,128)(2,1)S(1)} %get-tuple-element.49, bf16[128,512]{1,0:T(8,128)(2,1)S(1)} %get-tuple-element.48), kind=kOutput, calls=%fused_computation.32 | convolution fusion | flops 1075838976 | bytes 6815744 | tf_op jit(solution)/shard_map/dot_general | solution.py:82
  42.3 3.2 %fusion.5 = bf16[512,2048]{1,0:T(8,128)(2,1)S(1)} fusion(f32[512,2048]{1,0:T(8,128)S(1)} %fusion.16, bf16[512,2048]{1,0:T(8,128)(2,1)S(1)} %constant_dynamic-update-slice_fusion, bf16[512,128]{1,0:T(8,128)(2,1)S(1)} %get-tuple-element.46, bf16[512,128]{1,0:T(8,128)(2,1)S(1)} %get-tuple-element.47, bf16[512,128]{1,0:T(8,128)(2,1)S(1)} %get-tuple-element.45, ...), kind=kOutput, calls=%fused_computation.6 | convolution fusion | flops 1086324736 | bytes 8912896 | tf_op jit(solution)/shard_map/dot_general | solution.py:88
  48.6 1.8 collective-permute-start.11
  51.2 6.6 %collective-permute-done.11 = bf16[64,2048]{1,0:T(8,128)(2,1)S(1)} collective-permute-done((bf16[64,2048]{1,0:T(8,128)(2,1)S(1)}, bf16[64,2048]{1,0:T(8,128)(2,1)S(1)}, u32[]{:S(2)}, u32[]{:S(2)}) %collective-permute-start.11) | collective-permute-done | bytes 262176 | tf_op jit(solution)/shard_map/ppermute | solution.py:163
  57.8 5.1 %collective-permute-done.8 = bf16[64,2048]{1,0:T(8,128)(2,1)S(1)} collective-permute-done((bf16[64,2048]{1,0:T(8,128)(2,1)S(1)}, bf16[64,2048]{1,0:T(8,128)(2,1)S(1)}, u32[]{:S(2)}, u32[]{:S(2)}) %collective-permute-start.8) | collective-permute-done | bytes 262176 | tf_op jit(solution)/shard_map/ppermute | solution.py:163
  64.6 4.6 %collective-permute-start.12 = (bf16[64,15,128]{2,1,0:T(8,128)(2,1)S(1)}, bf16[64,15,128]{2,1,0:T(8,128)(2,1)S(1)}, u32[]{:S(2)}, u32[]{:S(2)}) collective-permute-start(bf16[64,15,128]{2,1,0:T(8,128)(2,1)S(1)} %get-tuple-element.54), channel_id=1, source_target_pairs={{0,1},{1,2},{2,3},{4,5},{5,6},{6,7},{8,9},{9,10},{10,11},{12,13},{... | collective-permute-start | bytes 737288 | tf_op jit(solution)/shard_map/ppermute | solution.py:169
  70.5 4.7 %collective-permute-start.9 = (bf16[64,15,128]{2,1,0:T(8,128)(2,1)S(1)}, bf16[64,15,128]{2,1,0:T(8,128)(2,1)S(1)}, u32[]{:S(2)}, u32[]{:S(2)}) collective-permute-start(bf16[64,15,128]{2,1,0:T(8,128)(2,1)S(1)} %get-tuple-element.52), channel_id=1, source_target_pairs={{0,1},{1,2},{2,3},{4,5},{5,6},{6,7},{8,9},{9,10},{10,11},{12,13},{... | collective-permute-start | bytes 737288 | tf_op jit(solution)/shard_map/ppermute | solution.py:169
  75.2 2.5 fusion.6
  80.6 13.7 %shard_map.94 = (f32[64,16,128]{2,1,0:T(8,128)S(1)}, f32[64,1536]{1,0:T(8,128)S(1)}) custom-call(bf16[64,48,128]{2,1,0:T(8,128)(2,1)S(1)} %get-tuple-element.57.rim_ref, bf16[64,16,128]{2,1,0:T(8,128)(2,1)S(1)} %slice.75.feat_ref, bf16[64,16,128]{2,1,0:T(8,128)(2,1)S(1)} %get-tuple-element.39.grad_ref, f32[64,1536]{1,0:T(8,128)S(1)} %get-tuple-element.37.base_ref), custom_call_target="tpu_custom_call" | custom-call | flops 6442450944 | bytes 2621440 | tf_op jit(solution)/shard_map/pallas_call | solution.py:57
  95.8 13.7 %shard_map.93 = (f32[64,16,128]{2,1,0:T(8,128)S(1)}, f32[64,1536]{1,0:T(8,128)S(1)}) custom-call(bf16[64,48,128]{2,1,0:T(8,128)(2,1)S(1)} %get-tuple-element.56.rim_ref, bf16[64,16,128]{2,1,0:T(8,128)(2,1)S(1)} %slice.67.feat_ref, bf16[64,16,128]{2,1,0:T(8,128)(2,1)S(1)} %get-tuple-element.38.grad_ref, f32[64,1536]{1,0:T(8,128)S(1)} %get-tuple-element.36.base_ref), custom_call_target="tpu_custom_call" | custom-call | flops 6442450944 | bytes 2621440 | tf_op jit(solution)/shard_map/pallas_call | solution.py:57
  109.5 1.6 reshape.35
  111.2 3.6 %fusion.34 = f32[512,512]{1,0:T(8,128)S(1)} fusion(bf16[512,2048]{1,0:T(8,128)(2,1)} %constant_dynamic-update-slice_fusion.4, bf16[512,2048]{1,0:T(8,128)(2,1)} %copy-done), kind=kOutput, calls=%fused_computation.79 | convolution fusion | flops 1073741824 | bytes 5242880 | tf_op jit(solution)/shard_map/dot_general | solution.py:76
  118.2 82.5 %all-reduce.5.cloned.1.call-done = (f32[64,31,31]{2,1,0:T(8,128)}, f32[64,31,31]{2,1,0:T(8,128)}) async-done(((f32[64,31,31]{2,1,0:T(8,128)}, f32[64,31,31]{2,1,0:T(8,128)}), (f32[64,31,31]{2,1,0:T(8,128)}, f32[64,31,31]{2,1,0:T(8,128)})) %all-reduce.5.cloned.1.call-update) | async-done | bytes 492048 | tf_op jit(solution)/shard_map/psum | solution.py:183
  200.7 1.9 copy.20
  204.7 24.5 %reduce-scatter.5.cloned.1.call-done = f32[512,128]{1,0:T(8,128)} async-done(((f32[512,512]{1,0:T(8,128)}), f32[512,128]{1,0:T(8,128)}) %reduce-scatter.5.cloned.1.call-update) | async-done | bytes 262160 | tf_op jit(solution)/shard_map/reduce_scatter | solution.py:196
  231.0 26.3 %reduce-scatter.3.cloned.1.call-done = f32[512,128]{1,0:T(8,128)} async-done(((f32[512,512]{1,0:T(8,128)}), f32[512,128]{1,0:T(8,128)}) %reduce-scatter.3.cloned.1.call-update) | async-done | bytes 262160 | tf_op jit(solution)/shard_map/reduce_scatter | solution.py:193
  257.3 1.7 broadcast_multiply_fusion.1
  (87 shorter events, 27.5 us)
Async XLA Ops:
  7.2 7.6 %copy-start.2 = (bf16[128,16,128]{2,1,0:T(8,128)(2,1)S(1)}, bf16[128,16,128]{2,1,0:T(8,128)(2,1)}, u32[]{:S(2)}) copy-start(bf16[128,16,128]{2,1,0:T(8,128)(2,1)} %param.7) | copy-start | bytes 1572868
  7.2 8.5 %copy-start.7 = (bf16[128,31,31]{0,2,1:T(8,128)(2,1)S(1)}, bf16[128,31,31]{0,2,1:T(8,128)(2,1)}, u32[]{:S(2)}) copy-start(bf16[128,31,31]{0,2,1:T(8,128)(2,1)} %param.9) | copy-start | bytes 738052
  7.2 193.5 %all-reduce.5.cloned.1.call-start = ((), (), s32[]{:S(2)}) async-start(), calls=%async_computation.4 | async-start | bytes 4194304 | tf_op jit(solution)/shard_map/psum | solution.py:183
  9.3 16.1 %collective-permute-start.3 = (bf16[128,2048]{1,0:T(8,128)(2,1)}, bf16[128,2048]{1,0:T(8,128)(2,1)}, u32[]{:S(2)}, u32[]{:S(2)}) collective-permute-start(bf16[128,2048]{1,0:T(8,128)(2,1)} %bitcast.35), channel_id=1, source_target_pairs={{0,4},{4,0},{8,12},{12,8},{1,5},{5,1},{9,13},{13,9},{2,6},{6,2},{1... | collective-permute-start | bytes 1572872 | tf_op jit(solution)/shard_map/ppermute | solution.py:113
  9.7 15.6 %collective-permute-start.4 = (bf16[128,2048]{1,0:T(8,128)(2,1)}, bf16[128,2048]{1,0:T(8,128)(2,1)}, u32[]{:S(2)}, u32[]{:S(2)}) collective-permute-start(bf16[128,2048]{1,0:T(8,128)(2,1)} %bitcast.35), channel_id=1, source_target_pairs={{0,8},{4,12},{8,0},{12,4},{1,9},{5,13},{9,1},{13,5},{2,10},{6,14},... | collective-permute-start | bytes 1572872 | tf_op jit(solution)/shard_map/ppermute | solution.py:123
  14.2 22.2 %collective-permute-start = (bf16[128,2048]{1,0:T(8,128)(2,1)}, bf16[128,2048]{1,0:T(8,128)(2,1)}, u32[]{:S(2)}, u32[]{:S(2)}) collective-permute-start(bf16[128,2048]{1,0:T(8,128)(2,1)} %bitcast.36), channel_id=1, source_target_pairs={{0,4},{4,0},{8,12},{12,8},{1,5},{5,1},{9,13},{13,9},{2,6},{6,2},{1... | collective-permute-start | bytes 1572872 | tf_op jit(solution)/shard_map/ppermute | solution.py:113
  14.5 21.9 %collective-permute-start.1 = (bf16[128,2048]{1,0:T(8,128)(2,1)}, bf16[128,2048]{1,0:T(8,128)(2,1)}, u32[]{:S(2)}, u32[]{:S(2)}) collective-permute-start(bf16[128,2048]{1,0:T(8,128)(2,1)} %bitcast.36), channel_id=1, source_target_pairs={{0,8},{4,12},{8,0},{12,4},{1,9},{5,13},{9,1},{13,5},{2,10},{6,14},... | collective-permute-start | bytes 1572872 | tf_op jit(solution)/shard_map/ppermute | solution.py:123
  16.3 1.2 copy-start.1
  19.8 16.6 %copy-start.8 = (bf16[512,2048]{1,0:T(8,128)(2,1)S(1)}, bf16[512,2048]{1,0:T(8,128)(2,1)}, u32[]{:S(2)}) copy-start(bf16[512,2048]{1,0:T(8,128)(2,1)} %constant_dynamic-update-slice_fusion.3) | copy-start | bytes 6291460
  25.3 13.2 %collective-permute-start.5 = (bf16[128,2048]{1,0:T(8,128)(2,1)}, bf16[128,2048]{1,0:T(8,128)(2,1)S(1)}, u32[]{:S(2)}, u32[]{:S(2)}) collective-permute-start(bf16[128,2048]{1,0:T(8,128)(2,1)} %collective-permute-done.4), channel_id=1, source_target_pairs={{0,4},{4,0},{8,12},{12,8},{1,5},{5,1},{9,13},{13,9},{2,6},{6,2},{1... | collective-permute-start | bytes 1572872 | tf_op jit(solution)/shard_map/ppermute | solution.py:113
  36.4 5.9 %collective-permute-start.2 = (bf16[128,2048]{1,0:T(8,128)(2,1)}, bf16[128,2048]{1,0:T(8,128)(2,1)S(1)}, u32[]{:S(2)}, u32[]{:S(2)}) collective-permute-start(bf16[128,2048]{1,0:T(8,128)(2,1)} %collective-permute-done.1), channel_id=1, source_target_pairs={{0,4},{4,0},{8,12},{12,8},{1,5},{5,1},{9,13},{13,9},{2,6},{6,2},{1... | collective-permute-start | bytes 1572872 | tf_op jit(solution)/shard_map/ppermute | solution.py:113
  45.5 5.7 %copy-start = (bf16[512,2048]{1,0:T(8,128)(2,1)}, bf16[512,2048]{1,0:T(8,128)(2,1)S(1)}, u32[]{:S(2)}) copy-start(bf16[512,2048]{1,0:T(8,128)(2,1)S(1)} %fusion.5) | copy-start | bytes 6291460
  46.0 2.1 collective-permute-start.7
  47.0 3.7 %collective-permute-start.6 = (bf16[128,2048]{1,0:T(8,128)(2,1)S(1)}, bf16[128,2048]{1,0:T(8,128)(2,1)S(1)}, u32[]{:S(2)}, u32[]{:S(2)}) collective-permute-start(bf16[128,2048]{1,0:T(8,128)(2,1)S(1)} %convolution_convert_fusion.1), channel_id=1, source_target_pairs={{0,4},{4,0},{8,12},{12,8},{1,5},{5,1},{9,13},{13,9},{2,6},{6,2},{1... | collective-permute-start | bytes 1572872 | tf_op jit(solution)/shard_map/ppermute | solution.py:113
  48.6 9.2 %collective-permute-start.11 = (bf16[64,2048]{1,0:T(8,128)(2,1)S(1)}, bf16[64,2048]{1,0:T(8,128)(2,1)S(1)}, u32[]{:S(2)}, u32[]{:S(2)}) collective-permute-start(bf16[64,2048]{1,0:T(8,128)(2,1)S(1)} %get-tuple-element.43), channel_id=1, source_target_pairs={{0,8},{4,12},{8,0},{12,4},{1,9},{5,13},{9,1},{13,5},{2,10},{6,14},... | collective-permute-start | bytes 786440 | tf_op jit(solution)/shard_map/ppermute | solution.py:163
  50.4 12.4 %collective-permute-start.8 = (bf16[64,2048]{1,0:T(8,128)(2,1)S(1)}, bf16[64,2048]{1,0:T(8,128)(2,1)S(1)}, u32[]{:S(2)}, u32[]{:S(2)}) collective-permute-start(bf16[64,2048]{1,0:T(8,128)(2,1)S(1)} %get-tuple-element.42), channel_id=1, source_target_pairs={{0,8},{4,12},{8,0},{12,4},{1,9},{5,13},{9,1},{13,5},{2,10},{6,14},... | collective-permute-start | bytes 786440 | tf_op jit(solution)/shard_map/ppermute | solution.py:163
  63.1 14.6 %collective-permute-start.10 = (bf16[64,15,128]{2,1,0:T(8,128)(2,1)S(1)}, bf16[64,15,128]{2,1,0:T(8,128)(2,1)S(1)}, u32[]{:S(2)}, u32[]{:S(2)}) collective-permute-start(bf16[64,15,128]{2,1,0:T(8,128)(2,1)S(1)} %get-tuple-element.53), channel_id=1, source_target_pairs={{1,0},{2,1},{3,2},{5,4},{6,5},{7,6},{9,8},{10,9},{11,10},{13,12},{... | collective-permute-start | bytes 737288 | tf_op jit(solution)/shard_map/ppermute | solution.py:170
  64.6 13.1 %collective-permute-start.12 = (bf16[64,15,128]{2,1,0:T(8,128)(2,1)S(1)}, bf16[64,15,128]{2,1,0:T(8,128)(2,1)S(1)}, u32[]{:S(2)}, u32[]{:S(2)}) collective-permute-start(bf16[64,15,128]{2,1,0:T(8,128)(2,1)S(1)} %get-tuple-element.54), channel_id=1, source_target_pairs={{0,1},{1,2},{2,3},{4,5},{5,6},{6,7},{8,9},{9,10},{10,11},{12,13},{... | collective-permute-start | bytes 737288 | tf_op jit(solution)/shard_map/ppermute | solution.py:169
  69.2 9.3 %collective-permute-start.13 = (bf16[64,15,128]{2,1,0:T(8,128)(2,1)S(1)}, bf16[64,15,128]{2,1,0:T(8,128)(2,1)S(1)}, u32[]{:S(2)}, u32[]{:S(2)}) collective-permute-start(bf16[64,15,128]{2,1,0:T(8,128)(2,1)S(1)} %get-tuple-element.55), channel_id=1, source_target_pairs={{1,0},{2,1},{3,2},{5,4},{6,5},{7,6},{9,8},{10,9},{11,10},{13,12},{... | collective-permute-start | bytes 737288 | tf_op jit(solution)/shard_map/ppermute | solution.py:170
  70.5 9.3 %collective-permute-start.9 = (bf16[64,15,128]{2,1,0:T(8,128)(2,1)S(1)}, bf16[64,15,128]{2,1,0:T(8,128)(2,1)S(1)}, u32[]{:S(2)}, u32[]{:S(2)}) collective-permute-start(bf16[64,15,128]{2,1,0:T(8,128)(2,1)S(1)} %get-tuple-element.52), channel_id=1, source_target_pairs={{0,1},{1,2},{2,3},{4,5},{5,6},{6,7},{8,9},{9,10},{10,11},{12,13},{... | collective-permute-start | bytes 737288 | tf_op jit(solution)/shard_map/ppermute | solution.py:169
  111.1 3.6 %copy-start.4 = (f32[512,512]{1,0:T(8,128)S(1)}, f32[512,512]{1,0:T(8,128)}, u32[]{:S(2)}) copy-start(f32[512,512]{1,0:T(8,128)} %fusion.6) | copy-start | bytes 3145732
  111.1 118.1 %reduce-scatter.5.cloned.1.call-start = ((), (), s32[]{:S(2)}) async-start(), calls=%async_computation.3 | async-start | bytes 1310720 | tf_op jit(solution)/shard_map/reduce_scatter | solution.py:196
  116.0 141.3 %reduce-scatter.3.cloned.1.call-start = ((), (), s32[]{:S(2)}) async-start(), calls=%async_computation.2 | async-start | bytes 1310720 | tf_op jit(solution)/shard_map/reduce_scatter | solution.py:193
  200.7 1.9 copy-start.3
  (2 other events, 2.1 us)
Sparse Core Ops, SparseCore 0:
  111.2 89.3 all-reduce.4
  203.1 26.0 reduce-scatter.4
  231.5 25.7 reduce-scatter.2

commit v2 on v1

--- a/solution.py
+++ b/solution.py
@@ -17,14 +17,15 @@
     return -(-count // unit) * unit
 
 
-def conv_kernel(size, rim_ref, feat_ref, grad_ref, base_ref, in_ref, part_ref):
-    group, depth, width = rim_ref.shape
-    rows = feat_ref.shape[1]
+def conv_kernel(size, take, low_ref, mid_ref, high_ref, feat_ref, grad_ref, base_ref, *rest):
+    in_ref, part_ref = rest[-2:]
+    group, rows, width = mid_ref.shape
+    depth = rows + 2 * take
     half = size // 2
     total = base_ref.shape[1]
     lane = lax.broadcasted_iota(jnp.int32, (depth, width), 1)
     for c in range(group):
-        rim = rim_ref[c]
+        rim = jnp.concatenate([low_ref[c], mid_ref[c], high_ref[c]], axis=0)
         pieces = []
         for b in range(size):
             shift = b - half
@@ -48,28 +49,34 @@
         part_ref[c : c + 1, :] = jnp.sum(aligned, axis=0, keepdims=True)
 
 
-def conv_back(rim, feat_reversed, grad, base, size):
-    channels, depth, width = rim.shape
-    rows = feat_reversed.shape[1]
+def conv_back(low, mid, high, feat_reversed, grad, base, earlier, start, size):
+    channels, rows, width = mid.shape
+    take = low.shape[1]
     total = base.shape[1]
     group = math.gcd(channels, GROUP)
-    block = lambda *dims: pl.BlockSpec((group,) + dims, lambda i: (i,) + (0,) * len(dims))
+    skip = start // group
+    own = lambda *dims: pl.BlockSpec((group,) + dims, lambda i: (i,) + (0,) * len(dims))
+    part = lambda *dims: pl.BlockSpec((group,) + dims, lambda i: (i + skip,) + (0,) * len(dims))
+    more = [] if earlier is None else [earlier]
     return pl.pallas_call(
-        functools.partial(conv_kernel, size),
+        functools.partial(conv_kernel, size, take),
         grid=(channels // group,),
         out_shape=(
-            jax.ShapeDtypeStruct((channels, rows, width), jnp.float32),
+            jax.ShapeDtypeStruct(grad.shape, jnp.float32),
             jax.ShapeDtypeStruct((channels, total), jnp.float32),
         ),
-        in_specs=[block(depth, width), block(rows, width), block(rows, width), block(total)],
-        out_specs=(block(rows, width), block(total)),
+        in_specs=[own(take, width), own(rows, width), own(take, width)]
+        + [part(rows, width), part(rows, width), part(total)]
+        + [pl.BlockSpec(memory_space=pl.ANY) for _ in more],
+        out_specs=(part(rows, width), own(total)),
+        input_output_aliases={6: 0} if more else {},
         compiler_params=pltpu.CompilerParams(vmem_limit_bytes=24 * 1024 * 1024),
         cost_estimate=pl.CostEstimate(
             flops=channels * rows * width * total * 4 * 8,
-            bytes_accessed=channels * width * (depth * 2 + rows * 8) + channels * total * 8,
+            bytes_accessed=channels * width * (rows * 14) + channels * total * 8,
             transcendentals=0,
         ),
-    )(rim, feat_reversed, grad, base)
+    )(low, mid, high, feat_reversed, grad, base, *more)
 
 
 def contract_last(left, right):
@@ -130,6 +137,18 @@
     w_out_own = jnp.concatenate(
         [lax.dynamic_slice_in_dim(w_out, at * local_ch, local_ch, 1) for at in owner], axis=1
     )
+    hops = lax.axis_size("sp")
+    depth_bits = hops.bit_length() - 1
+    mine = lax.axis_index("sp")
+    unit = w_in.shape[1] // hops
+    order = [sum(((p >> i) & 1) << (depth_bits - 1 - i) for i in range(depth_bits)) for p in range(hops)]
+    places = [jnp.bitwise_xor(mine, bits) * unit for bits in order]
+    w_in_own = jnp.concatenate(
+        [lax.dynamic_slice_in_dim(w_in_own, at, unit, 1) for at in places], axis=1
+    )
+    w_out_own = jnp.concatenate(
+        [lax.dynamic_slice_in_dim(w_out_own, at, unit, 0) for at in places], axis=0
+    )
     mixed_all = gathered(saved_mix.reshape(local_ch, local_pos))
     grad_all = gathered(out_grad.reshape(local_ch, local_pos))
     hidden, preact_grad = pointwise_back(mixed_all, grad_all, w_in_own, w_out_own)
@@ -144,17 +163,52 @@
     pieces = 2 if local_ch % 32 == 0 else 1
     chunk = local_ch // pieces
 
-    depth = up(rows + size - 1, 16)
+    w_in_sum, w_out_sum = None, None
+    span, bit = w_in.shape[1], 1
+    while bit < hops:
+        span //= 2
+        pairs = [(i, i ^ bit) for i in range(hops)]
+        trade = lambda value: lax.ppermute(value.astype(jnp.bfloat16), "sp", pairs).astype(jnp.float32)
+        if bit == 1:
+            w_in_away = trade(contract_last(mixed_all, preact_grad[span:]))
+            w_out_away = trade(contract_last(hidden[span:], grad_all))
+            w_in_sum = contract_last(mixed_all, preact_grad[:span]) + w_in_away
+            w_out_sum = contract_last(hidden[:span], grad_all) + w_out_away
+        else:
+            w_in_sum = w_in_sum[:, :span] + trade(w_in_sum[:, span:])
+            w_out_sum = w_out_sum[:span] + trade(w_out_sum[span:])
+        bit *= 2
+
+    take = min(rows, up(half, 16))
+    depth = rows + 2 * take
     total = up(size * depth, 128)
+    ahead = take - half
     flipped = kernel[:, ::-1, ::-1].astype(jnp.float32).transpose(0, 2, 1)
-    base = jnp.pad(flipped, ((0, 0), (0, 0), (0, depth - size))).reshape(local_ch, size * depth)
-    base = jnp.pad(base, ((0, 0), (0, total - size * depth)))
+    base = jnp.pad(flipped, ((0, 0), (0, 0), (ahead, depth - size - ahead)))
+    base = jnp.pad(base.reshape(local_ch, size * depth), ((0, 0), (0, total - size * depth)))
     feat_reversed = features[:, ::-1]
-    hops = lax.axis_size("sp")
     forward = [(i, i + 1) for i in range(hops - 1)]
     backward = [(i + 1, i) for i in range(hops - 1)]
 
-    in_grads, kernel_grads = [], []
+    def summed(lines):
+        each = lines.shape[0] // hops
+        shift = lambda step: [(i, (i + step) % hops) for i in range(hops)]
+        cut = lambda step: lax.dynamic_slice_in_dim(lines, lax.rem(mine + step, hops) * each, each, 0)
+        come = [
+            lax.ppermute(cut(step).astype(jnp.bfloat16), "sp", shift(step)) for step in range(1, hops)
+        ]
+        block = cut(0)
+        for value in come:
+            block = block + value.astype(jnp.float32)
+        whole = jnp.zeros_like(lines)
+        for step in range(hops):
+            value = block if step == 0 else lax.ppermute(block, "sp", shift(hops - step))
+            whole = lax.dynamic_update_slice_in_dim(
+                whole, value, lax.rem(mine + step, hops) * each, 0
+            )
+        return whole
+
+    in_grad, lines = None, []
     for piece in range(pieces):
         at = slice(piece * chunk, (piece + 1) * chunk)
         mix = pair[0][at]
@@ -162,43 +216,34 @@
             sent = pair[step][at].astype(jnp.bfloat16)
             mix = mix + lax.ppermute(sent, "ch", across(step)).astype(jnp.float32)
         mix = mix.astype(jnp.bfloat16).reshape(chunk, rows, width)
-        low, high, left = [], [], half
-        below, above = mix, mix
-        while left > 0:
-            take = min(left, rows)
-            below = lax.ppermute(below[:, rows - take :] if below.shape[1] >= take else below, "sp", forward)
-            above = lax.ppermute(above[:, :take], "sp", backward)
-            low.insert(0, below)
-            high.append(above)
-            left -= take
-        rim = jnp.concatenate(
-            low + [mix] + high + [jnp.zeros((chunk, depth - rows - size + 1, width), mix.dtype)],
-            axis=1,
+        low = lax.ppermute(mix[:, rows - take :], "sp", forward)
+        high = lax.ppermute(mix[:, :take], "sp", backward)
+        in_grad, line = conv_back(
+            low, mix, high, feat_reversed, out_grad, base, in_grad, piece * chunk, size
         )
-        in_part, kernel_part = conv_back(
-            rim, feat_reversed[at], out_grad[at], base[at], size
-        )
-        in_grads.append(in_part)
-        kernel_part = kernel_part[:, : size * depth].reshape(chunk, size, depth)[:, :, :size]
-        kernel_grads.append(lax.psum(kernel_part, "sp"))
-
-    def absolute(value):
+        lines.append(summed(line))
+
+    def absolute(value, dim):
         blocks = []
         for j in range(count):
             step = lax.rem(j // 2 - me // 2 + chips, chips)
             place = step * 2 + lax.rem(me + j, 2)
-            blocks.append(lax.dynamic_slice_in_dim(value, place * local_ch, local_ch, 0))
-        return jnp.concatenate(blocks, axis=0)
-
-    w_in_sum = lax.psum_scatter(
-        absolute(contract_last(mixed_all, preact_grad)), "sp", scatter_dimension=1, tiled=True
-    )
-    w_out_sum = lax.psum_scatter(
-        absolute(contract_last(grad_all, hidden)), "sp", scatter_dimension=1, tiled=True
-    )
-    in_grad = jnp.concatenate(in_grads, axis=0)
-    kernel_grad = jnp.concatenate(kernel_grads, axis=0).transpose(0, 2, 1)[:, ::-1, ::-1] * factor
-    return (in_grad, kernel_grad, w_in_sum * factor, w_out_sum.T * factor)
+            blocks.append(lax.dynamic_slice_in_dim(value, place * local_ch, local_ch, dim))
+        return jnp.concatenate(blocks, axis=dim)
+
+    kernel_grad = [
+        line[:, : size * depth]
+        .reshape(-1, size, depth)[:, :, ahead : ahead + size]
+        .transpose(0, 2, 1)[:, ::-1, ::-1]
+        for line in lines
+    ]
+    kernel_grad = jnp.concatenate(kernel_grad, axis=0) * factor
+    return (
+        in_grad,
+        kernel_grad,
+        absolute(w_in_sum, 0) * factor,
+        absolute(w_out_sum, 1) * factor,
+    )
 
 
 def solution(mesh):

time: 266 us -> 160 us (0.60)
  waiting for transfers between devices: 161 us -> 51 us
  starting transfers between devices: 18.3 us -> 40.7 us
  between operations: 14.2 us -> 1.34 us
  other arithmetic: 6.99 us -> 3.9 us
    psum x1 -> x0, waiting for transfers between devices: 82.5 us -> none  [per_device(): kernel_grads.append(lax.psum(kernel_part, 'sp'))]
    reduce_scatter x2 -> x0, waiting for transfers between devices: 50.8 us -> none  [the longest x1 26.3 us: per_device(): lax.psum_scatter(absolute(contract_last(mixed_all, preact_grad)), 'sp', s...]
    ppermute x4 -> x20, waiting for transfers between devices: 2.09 us -> 27.8 us  [the longest x4 18.6 us: per_device(): lax.ppermute(value.astype(jnp.bfloat16), 'sp', pairs).astype(jnp.float32)]
    ppermute x4 -> x20, starting transfers between devices: 11.9 us -> 34.5 us  [the longest x6 10.8 us: summed(): lax.ppermute(block, 'sp', shift(hops - step))]
    rev x1 -> x5, local copies, waits for them, and re-layouts: 0.16 us -> 3.87 us  [the longest x4 3.62 us: per_device(): line[:, :size * depth].reshape(-1, size, depth)[:, :, ahead:ahead + size]]
    dot_general x2 -> x4, matrix products: 6.08 us -> 2.97 us  [contract_last(): lax.dot_general(left, right, (((1,), (1,)), ((), ())), preferred_element_...]
    concatenate x4 -> x3, other arithmetic: 3.9 us -> 1.12 us  [the longest x1 1.03 us: per_device(): jnp.concatenate([lax.dynamic_slice_in_dim(w_in_own, at, unit, 1) for at i...]
    unnamed x31 -> x43, local copies, waits for them, and re-layouts: 14.9 us -> 12.6 us
  transfers between devices with their start and end apart: 17 -> 30, of which waited for: 10 -> 13; matrix products, arithmetic and copies ran while one was open for 12% -> 17% of each run, Pallas kernels for 0% -> 9%
where the time goes in v2:
time: 160 us
  waiting for transfers between devices  51 us (32%)
  starting transfers between devices  40.7 us (25%)
  Pallas kernels  28.5 us (18%)
  local copies, waits for them, and re-layouts  21.5 us (13%)
  matrix products  12.6 us (8%)
  other arithmetic  3.9 us (2%)
    pallas_call x2, Pallas kernels, conv_back(): pl.pallas_call(functools.partial(conv_kernel, size, take), grid=(channels...  28.5 us
    ppermute x4, waiting for transfers between devices, per_device(): lax.ppermute(value.astype(jnp.bfloat16), 'sp', pairs).astype(jnp.float32)  18.6 us
    unnamed x43, local copies, waits for them, and re-layouts  12.6 us
    ppermute x2, waiting for transfers between devices, gathered(): lax.ppermute(block, 'ch', across(chips - step))  11.9 us
    ppermute x2, waiting for transfers between devices, per_device(): mix = mix + lax.ppermute(sent, 'ch', across(step)).astype(jnp.float32)  11.3 us
    ppermute x6, starting transfers between devices, summed(): lax.ppermute(block, 'sp', shift(hops - step))  10.8 us
    ppermute x6, starting transfers between devices, summed(): lax.ppermute(cut(step).astype(jnp.bfloat16), 'sp', shift(step))  9.53 us
    dot_general x5, matrix products, matmul(): return jnp.dot(left, right, preferred_element_type=jnp.float32)  6.17 us
  transfers between devices with their start and end apart: 30, of which 13 were waited for; matrix products, arithmetic and copies ran while one was open for 17% of the time, Pallas kernels for 9%

profile of v2, /device:TPU:0, one launch (start us, length us, event | category | flops | bytes accessed | tf_op | source)
XLA Modules:
  0.0 159.6 jit_solution(11832806420835354103)
XLA Ops:
  0.7 2.1 %copy.29 = bf16[16,8,16,128]{3,1,2,0:T(8,128)(2,1)} copy(bf16[16,8,16,128]{3,2,1,0:T(8,128)(2,1)} %bitcast.44) | data formatting | bytes 1048576
  3.2 2.5 %collective-permute-start.4 = (bf16[128,2048]{1,0:T(8,128)(2,1)}, bf16[128,2048]{1,0:T(8,128)(2,1)}, u32[]{:S(2)}, u32[]{:S(2)}) collective-permute-start(bf16[128,2048]{1,0:T(8,128)(2,1)} %bitcast.32), channel_id=1, source_target_pairs={{0,8},{4,12},{8,0},{12,4},{1,9},{5,13},{9,1},{13,5},{2,10},{6,14},... | collective-permute-start | bytes 1572872 | tf_op jit(solution)/shard_map/ppermute | solution.py:130
  5.7 2.0 %copy.30 = bf16[16,8,16,128]{3,1,2,0:T(8,128)(2,1)} copy(bf16[16,8,16,128]{3,2,1,0:T(8,128)(2,1)} %bitcast.36) | data formatting | bytes 1048576
  14.0 4.8 %collective-permute-done.4 = bf16[128,2048]{1,0:T(8,128)(2,1)} collective-permute-done((bf16[128,2048]{1,0:T(8,128)(2,1)}, bf16[128,2048]{1,0:T(8,128)(2,1)}, u32[]{:S(2)}, u32[]{:S(2)}) %collective-permute-start.4) | collective-permute-done | bytes 524320 | tf_op jit(solution)/shard_map/ppermute | solution.py:130
  20.7 1.9 %constant_dynamic-update-slice_fusion.5 = bf16[512,2048]{1,0:T(8,128)(2,1)} fusion(bf16[512,2048]{1,0:T(8,128)(2,1)} %constant_dynamic-update-slice_fusion.6, bf16[128,2048]{1,0:T(8,128)(2,1)} %collective-permute-done.4), kind=kLoop, calls=%fused_computation.68 | loop fusion | bytes 1048576
  22.6 7.1 %collective-permute-done.1 = bf16[128,2048]{1,0:T(8,128)(2,1)S(1)} collective-permute-done((bf16[128,2048]{1,0:T(8,128)(2,1)}, bf16[128,2048]{1,0:T(8,128)(2,1)S(1)}, u32[]{:S(2)}, u32[]{:S(2)}) %collective-permute-start.1) | collective-permute-done | bytes 524320 | tf_op jit(solution)/shard_map/ppermute | solution.py:130
  33.4 3.5 %multiply_convert_fusion = (bf16[512,2048]{1,0:T(8,128)(2,1)S(1)}, f32[512,2048]{1,0:T(8,128)S(1)}) fusion(bf16[512,2048]{1,0:T(8,128)(2,1)} %constant_dynamic-update-slice_fusion.4, bf16[512,128]{1,0:T(8,128)(2,1)S(1)} %copy-done.6, bf16[512,128]{1,0:T(8,128)(2,1)S(1)} %copy-done.7, bf16[512,128]{1,0:T(8,128)(2,1)S(1)} %copy-done.8, ...), kind=kOutput, calls=%fused_computation.7 | convolution fusion | flops 1081081856 | bytes 8912896 | tf_op jit(solution)/shard_map/dot_general | solution.py:89
  37.0 4.3 %fusion.5 = bf16[512,2048]{1,0:T(8,128)(2,1)S(1)} fusion(f32[512,2048]{1,0:T(8,128)S(1)} %get-tuple-element.55, bf16[512,2048]{1,0:T(8,128)(2,1)S(1)} %constant_dynamic-update-slice_fusion, bf16[128,512]{1,0:T(8,128)(2,1)S(1)} %copy-done.13, bf16[128,512]{1,0:T(8,128)(2,1)S(1)} %copy-done.14, bf16[128,512]{1,0:T(8,128)(2,1)S(1)} %copy-done.15, ...), kind=kOutput, calls=%fused_computation.6 | convolution fusion | flops 1086324736 | bytes 8912896 | tf_op jit(solution)/shard_map/dot_general | solution.py:95
  46.6 6.2 %collective-permute-done.28 = bf16[256,512]{1,0:T(8,128)(2,1)S(1)} collective-permute-done((bf16[256,512]{1,0:T(8,128)(2,1)S(1)}, bf16[256,512]{1,0:T(8,128)(2,1)S(1)}, u32[]{:S(2)}, u32[]{:S(2)}) %collective-permute-start.28) | collective-permute-done | bytes 262176 | tf_op jit(solution)/shard_map/ppermute | solution.py:171
  53.6 2.9 %collective-permute-start.29 = (bf16[128,512]{1,0:T(8,128)(2,1)S(1)}, bf16[128,512]{1,0:T(8,128)(2,1)S(1)}, u32[]{:S(2)}, u32[]{:S(2)}) collective-permute-start(bf16[128,512]{1,0:T(8,128)(2,1)S(1)} %slice.140), channel_id=1, source_target_pairs={{0,2},{1,3},{2,0},{3,1},{4,6},{5,7},{6,4},{7,5},{8,10},{9,11},{10,... | collective-permute-start | bytes 393224 | tf_op jit(solution)/shard_map/ppermute | solution.py:171
  56.5 4.4 %collective-permute-done.26 = bf16[512,256]{1,0:T(8,128)(2,1)S(1)} collective-permute-done((bf16[512,256]{1,0:T(8,128)(2,1)S(1)}, bf16[512,256]{1,0:T(8,128)(2,1)S(1)}, u32[]{:S(2)}, u32[]{:S(2)}) %collective-permute-start.26) | collective-permute-done | bytes 262176 | tf_op jit(solution)/shard_map/ppermute | solution.py:171
  62.2 8.0 %collective-permute-done.27 = bf16[512,128]{1,0:T(8,128)(2,1)S(1)} collective-permute-done((bf16[512,128]{1,0:T(8,128)(2,1)S(1)}, bf16[512,128]{1,0:T(8,128)(2,1)S(1)}, u32[]{:S(2)}, u32[]{:S(2)}) %collective-permute-start.27) | collective-permute-done | bytes 131104 | tf_op jit(solution)/shard_map/ppermute | solution.py:171
  73.3 6.6 %collective-permute-done.11 = bf16[64,2048]{1,0:T(8,128)(2,1)S(1)} collective-permute-done((bf16[64,2048]{1,0:T(8,128)(2,1)S(1)}, bf16[64,2048]{1,0:T(8,128)(2,1)S(1)}, u32[]{:S(2)}, u32[]{:S(2)}) %collective-permute-start.11) | collective-permute-done | bytes 262176 | tf_op jit(solution)/shard_map/ppermute | solution.py:217
  80.0 4.7 %collective-permute-done.8 = bf16[64,2048]{1,0:T(8,128)(2,1)S(1)} collective-permute-done((bf16[64,2048]{1,0:T(8,128)(2,1)S(1)}, bf16[64,2048]{1,0:T(8,128)(2,1)S(1)}, u32[]{:S(2)}, u32[]{:S(2)}) %collective-permute-start.8) | collective-permute-done | bytes 262176 | tf_op jit(solution)/shard_map/ppermute | solution.py:217
  89.0 4.6 %collective-permute-start.9 = (bf16[64,16,128]{2,1,0:T(8,128)(2,1)S(1)}, bf16[64,16,128]{2,1,0:T(8,128)(2,1)S(1)}, u32[]{:S(2)}, u32[]{:S(2)}) collective-permute-start(bf16[64,16,128]{2,1,0:T(8,128)(2,1)S(1)} %bitcast.41), channel_id=1, source_target_pairs={{0,1},{1,2},{2,3},{4,5},{5,6},{6,7},{8,9},{9,10},{10,11},{12,13},{... | collective-permute-start | bytes 786440 | tf_op jit(solution)/shard_map/ppermute | solution.py:219
  95.4 14.2 %shard_map.93 = (f32[128,16,128]{2,1,0:T(8,128)}, f32[64,1536]{1,0:T(8,128)S(1)}) custom-call(bf16[64,16,128]{2,1,0:T(8,128)(2,1)S(1)} %collective-permute-done.12.low_ref, bf16[64,16,128]{2,1,0:T(8,128)(2,1)S(1)} %bitcast.40, bf16[64,16,128]{2,1,0:T(8,128)(2,1)S(1)} %collective-permute-done.13.high_ref, bf16[128,16,128]{2,1,0:T(8,128)(2,1)S(1)} %rev.12.feat_ref, ...), custom_call_target="tpu_custom_call" | custom-call | flops 6442450944 | bytes 2621440 | tf_op jit(solution)/shard_map/pallas_call | solution.py:61
  109.7 14.2 %shard_map.94 = (f32[128,16,128]{2,1,0:T(8,128)}, f32[64,1536]{1,0:T(8,128)S(1)}) custom-call(bf16[64,16,128]{2,1,0:T(8,128)(2,1)S(1)} %collective-permute-done.9.low_ref, bf16[64,16,128]{2,1,0:T(8,128)(2,1)S(1)} %bitcast.43, bf16[64,16,128]{2,1,0:T(8,128)(2,1)S(1)} %collective-permute-done.10.high_ref, ...), custom_call_target="tpu_custom_call", output_to_operand_aliasing={{0}: (6, {})} | custom-call | flops 6442450944 | bytes 2621440 | tf_op jit(solution)/shard_map/pallas_call | solution.py:61
  123.9 4.5 %collective-permute-start.22 = (bf16[16,1536]{1,0:T(8,128)(2,1)S(1)}, bf16[16,1536]{1,0:T(8,128)(2,1)S(1)}, u32[]{:S(2)}, u32[]{:S(2)}) collective-permute-start(bf16[16,1536]{1,0:T(8,128)(2,1)S(1)} %get-tuple-element.44), channel_id=1, source_target_pairs={{0,3},{1,0},{2,1},{3,2},{4,7},{5,4},{6,5},{7,6},{8,11},{9,8},{10,9... | collective-permute-start | bytes 147464 | tf_op jit(solution)/shard_map/ppermute | solution.py:198
  129.1 3.2 %collective-permute-start.16 = (bf16[16,1536]{1,0:T(8,128)(2,1)S(1)}, bf16[16,1536]{1,0:T(8,128)(2,1)S(1)}, u32[]{:S(2)}, u32[]{:S(2)}) collective-permute-start(bf16[16,1536]{1,0:T(8,128)(2,1)S(1)} %get-tuple-element.41), channel_id=1, source_target_pairs={{0,3},{1,0},{2,1},{3,2},{4,7},{5,4},{6,5},{7,6},{8,11},{9,8},{10,9... | collective-permute-start | bytes 147464 | tf_op jit(solution)/shard_map/ppermute | solution.py:198
  134.6 2.8 %collective-permute-start.23 = (f32[16,1536]{1,0:T(8,128)S(1)}, f32[16,1536]{1,0:T(8,128)S(1)}, u32[]{:S(2)}, u32[]{:S(2)}) collective-permute-start(f32[16,1536]{1,0:T(8,128)S(1)} %get-tuple-element.19), channel_id=1, source_target_pairs={{0,3},{1,0},{2,1},{3,2},{4,7},{5,4},{6,5},{7,6},{8,11},{9,8},{10,9... | collective-permute-start | bytes 294920 | tf_op jit(solution)/shard_map/ppermute | solution.py:205
  138.4 2.4 %collective-permute-done.15 = bf16[16,1536]{1,0:T(8,128)(2,1)S(1)} collective-permute-done((bf16[16,1536]{1,0:T(8,128)(2,1)S(1)}, bf16[16,1536]{1,0:T(8,128)(2,1)S(1)}, u32[]{:S(2)}, u32[]{:S(2)}) %collective-permute-start.15) | collective-permute-done | bytes 49184 | tf_op jit(solution)/shard_map/ppermute | solution.py:198
  141.7 4.2 %collective-permute-start.18 = (f32[16,1536]{1,0:T(8,128)S(1)}, f32[16,1536]{1,0:T(8,128)S(1)}, u32[]{:S(2)}, u32[]{:S(2)}) collective-permute-start(f32[16,1536]{1,0:T(8,128)S(1)} %get-tuple-element.17), channel_id=1, source_target_pairs={{0,2},{1,3},{2,0},{3,1},{4,6},{5,7},{6,4},{7,5},{8,10},{9,11},{10,... | collective-permute-start | bytes 294920 | tf_op jit(solution)/shard_map/ppermute | solution.py:205
  145.9 1.9 %collective-permute-start.19 = (f32[16,1536]{1,0:T(8,128)S(1)}, f32[16,1536]{1,0:T(8,128)S(1)}, u32[]{:S(2)}, u32[]{:S(2)}) collective-permute-start(f32[16,1536]{1,0:T(8,128)S(1)} %get-tuple-element.17), channel_id=1, source_target_pairs={{0,1},{1,2},{2,3},{3,0},{4,5},{5,6},{6,7},{7,4},{8,9},{9,10},{10,1... | collective-permute-start | bytes 294920 | tf_op jit(solution)/shard_map/ppermute | solution.py:205
  150.1 4.0 %collective-permute-done.18 = f32[16,1536]{1,0:T(8,128)S(1)} collective-permute-done((f32[16,1536]{1,0:T(8,128)S(1)}, f32[16,1536]{1,0:T(8,128)S(1)}, u32[]{:S(2)}, u32[]{:S(2)}) %collective-permute-start.18) | collective-permute-done | bytes 98336 | tf_op jit(solution)/shard_map/ppermute | solution.py:205
  (135 shorter events, 41.2 us)
Async XLA Ops:
  2.7 16.1 %collective-permute-start.3 = (bf16[128,2048]{1,0:T(8,128)(2,1)}, bf16[128,2048]{1,0:T(8,128)(2,1)}, u32[]{:S(2)}, u32[]{:S(2)}) collective-permute-start(bf16[128,2048]{1,0:T(8,128)(2,1)} %bitcast.32), channel_id=1, source_target_pairs={{0,4},{4,0},{8,12},{12,8},{1,5},{5,1},{9,13},{13,9},{2,6},{6,2},{1... | collective-permute-start | bytes 1572872 | tf_op jit(solution)/shard_map/ppermute | solution.py:120
  3.2 15.6 %collective-permute-start.4 = (bf16[128,2048]{1,0:T(8,128)(2,1)}, bf16[128,2048]{1,0:T(8,128)(2,1)}, u32[]{:S(2)}, u32[]{:S(2)}) collective-permute-start(bf16[128,2048]{1,0:T(8,128)(2,1)} %bitcast.32), channel_id=1, source_target_pairs={{0,8},{4,12},{8,0},{12,4},{1,9},{5,13},{9,1},{13,5},{2,10},{6,14},... | collective-permute-start | bytes 1572872 | tf_op jit(solution)/shard_map/ppermute | solution.py:130
  7.7 22.1 %collective-permute-start = (bf16[128,2048]{1,0:T(8,128)(2,1)}, bf16[128,2048]{1,0:T(8,128)(2,1)}, u32[]{:S(2)}, u32[]{:S(2)}) collective-permute-start(bf16[128,2048]{1,0:T(8,128)(2,1)} %bitcast.33), channel_id=1, source_target_pairs={{0,4},{4,0},{8,12},{12,8},{1,5},{5,1},{9,13},{13,9},{2,6},{6,2},{1... | collective-permute-start | bytes 1572872 | tf_op jit(solution)/shard_map/ppermute | solution.py:120
  7.9 21.8 %collective-permute-start.1 = (bf16[128,2048]{1,0:T(8,128)(2,1)}, bf16[128,2048]{1,0:T(8,128)(2,1)S(1)}, u32[]{:S(2)}, u32[]{:S(2)}) collective-permute-start(bf16[128,2048]{1,0:T(8,128)(2,1)} %bitcast.33), channel_id=1, source_target_pairs={{0,8},{4,12},{8,0},{12,4},{1,9},{5,13},{9,1},{13,5},{2,10},{6,14},... | collective-permute-start | bytes 1572872 | tf_op jit(solution)/shard_map/ppermute | solution.py:130
  18.8 13.7 %collective-permute-start.5 = (bf16[128,2048]{1,0:T(8,128)(2,1)}, bf16[128,2048]{1,0:T(8,128)(2,1)S(1)}, u32[]{:S(2)}, u32[]{:S(2)}) collective-permute-start(bf16[128,2048]{1,0:T(8,128)(2,1)} %collective-permute-done.4), channel_id=1, source_target_pairs={{0,4},{4,0},{8,12},{12,8},{1,5},{5,1},{9,13},{13,9},{2,6},{6,2},{1... | collective-permute-start | bytes 1572872 | tf_op jit(solution)/shard_map/ppermute | solution.py:120
  42.2 28.0 %collective-permute-start.7 = (bf16[128,2048]{1,0:T(8,128)(2,1)S(1)}, bf16[128,2048]{1,0:T(8,128)(2,1)S(1)}, u32[]{:S(2)}, u32[]{:S(2)}) collective-permute-start(bf16[128,2048]{1,0:T(8,128)(2,1)S(1)} %convolution_convert_fusion), channel_id=1, source_target_pairs={{0,4},{4,0},{8,12},{12,8},{1,5},{5,1},{9,13},{13,9},{2,6},{6,2},{1... | collective-permute-start | bytes 1572872 | tf_op jit(solution)/shard_map/ppermute | solution.py:120
  42.8 30.0 %collective-permute-start.6 = (bf16[128,2048]{1,0:T(8,128)(2,1)S(1)}, bf16[128,2048]{1,0:T(8,128)(2,1)S(1)}, u32[]{:S(2)}, u32[]{:S(2)}) collective-permute-start(bf16[128,2048]{1,0:T(8,128)(2,1)S(1)} %convolution_convert_fusion.1), channel_id=1, source_target_pairs={{0,4},{4,0},{8,12},{12,8},{1,5},{5,1},{9,13},{13,9},{2,6},{6,2},{1... | collective-permute-start | bytes 1572872 | tf_op jit(solution)/shard_map/ppermute | solution.py:120
  43.6 9.2 %collective-permute-start.28 = (bf16[256,512]{1,0:T(8,128)(2,1)S(1)}, bf16[256,512]{1,0:T(8,128)(2,1)S(1)}, u32[]{:S(2)}, u32[]{:S(2)}) collective-permute-start(bf16[256,512]{1,0:T(8,128)(2,1)S(1)} %convolution_convert_fusion.2), channel_id=1, source_target_pairs={{0,1},{1,0},{2,3},{3,2},{4,5},{5,4},{6,7},{7,6},{8,9},{9,8},{10,11... | collective-permute-start | bytes 786440 | tf_op jit(solution)/shard_map/ppermute | solution.py:171
  46.3 14.6 %collective-permute-start.26 = (bf16[512,256]{1,0:T(8,128)(2,1)S(1)}, bf16[512,256]{1,0:T(8,128)(2,1)S(1)}, u32[]{:S(2)}, u32[]{:S(2)}) collective-permute-start(bf16[512,256]{1,0:T(8,128)(2,1)S(1)} %convolution_convert_fusion.3), channel_id=1, source_target_pairs={{0,1},{1,0},{2,3},{3,2},{4,5},{5,4},{6,7},{7,6},{8,9},{9,8},{10,11... | collective-permute-start | bytes 786440 | tf_op jit(solution)/shard_map/ppermute | solution.py:171
  53.6 8.5 %collective-permute-start.29 = (bf16[128,512]{1,0:T(8,128)(2,1)S(1)}, bf16[128,512]{1,0:T(8,128)(2,1)S(1)}, u32[]{:S(2)}, u32[]{:S(2)}) collective-permute-start(bf16[128,512]{1,0:T(8,128)(2,1)S(1)} %slice.140), channel_id=1, source_target_pairs={{0,2},{1,3},{2,0},{3,1},{4,6},{5,7},{6,4},{7,5},{8,10},{9,11},{10,... | collective-permute-start | bytes 393224 | tf_op jit(solution)/shard_map/ppermute | solution.py:171
  61.6 8.6 %collective-permute-start.27 = (bf16[512,128]{1,0:T(8,128)(2,1)S(1)}, bf16[512,128]{1,0:T(8,128)(2,1)S(1)}, u32[]{:S(2)}, u32[]{:S(2)}) collective-permute-start(bf16[512,128]{1,0:T(8,128)(2,1)S(1)} %slice.141), channel_id=1, source_target_pairs={{0,2},{1,3},{2,0},{3,1},{4,6},{5,7},{6,4},{7,5},{8,10},{9,11},{10,... | collective-permute-start | bytes 393224 | tf_op jit(solution)/shard_map/ppermute | solution.py:171
  70.7 9.2 %collective-permute-start.11 = (bf16[64,2048]{1,0:T(8,128)(2,1)S(1)}, bf16[64,2048]{1,0:T(8,128)(2,1)S(1)}, u32[]{:S(2)}, u32[]{:S(2)}) collective-permute-start(bf16[64,2048]{1,0:T(8,128)(2,1)S(1)} %get-tuple-element.22), channel_id=1, source_target_pairs={{0,8},{4,12},{8,0},{12,4},{1,9},{5,13},{9,1},{13,5},{2,10},{6,14},... | collective-permute-start | bytes 786440 | tf_op jit(solution)/shard_map/ppermute | solution.py:217
  72.3 12.3 %collective-permute-start.8 = (bf16[64,2048]{1,0:T(8,128)(2,1)S(1)}, bf16[64,2048]{1,0:T(8,128)(2,1)S(1)}, u32[]{:S(2)}, u32[]{:S(2)}) collective-permute-start(bf16[64,2048]{1,0:T(8,128)(2,1)S(1)} %get-tuple-element.23), channel_id=1, source_target_pairs={{0,8},{4,12},{8,0},{12,4},{1,9},{5,13},{9,1},{13,5},{2,10},{6,14},... | collective-permute-start | bytes 786440 | tf_op jit(solution)/shard_map/ppermute | solution.py:217
  84.8 10.2 %collective-permute-start.12 = (bf16[64,16,128]{2,1,0:T(8,128)(2,1)S(1)}, bf16[64,16,128]{2,1,0:T(8,128)(2,1)S(1)}, u32[]{:S(2)}, u32[]{:S(2)}) collective-permute-start(bf16[64,16,128]{2,1,0:T(8,128)(2,1)S(1)} %bitcast.38), channel_id=1, source_target_pairs={{0,1},{1,2},{2,3},{4,5},{5,6},{6,7},{8,9},{9,10},{10,11},{12,13},{... | collective-permute-start | bytes 786440 | tf_op jit(solution)/shard_map/ppermute | solution.py:219
  86.2 9.3 %collective-permute-start.13 = (bf16[64,16,128]{2,1,0:T(8,128)(2,1)S(1)}, bf16[64,16,128]{2,1,0:T(8,128)(2,1)S(1)}, u32[]{:S(2)}, u32[]{:S(2)}) collective-permute-start(bf16[64,16,128]{2,1,0:T(8,128)(2,1)S(1)} %bitcast.39), channel_id=1, source_target_pairs={{1,0},{2,1},{3,2},{5,4},{6,5},{7,6},{9,8},{10,9},{11,10},{13,12},{... | collective-permute-start | bytes 786440 | tf_op jit(solution)/shard_map/ppermute | solution.py:220
  89.0 20.6 %collective-permute-start.9 = (bf16[64,16,128]{2,1,0:T(8,128)(2,1)S(1)}, bf16[64,16,128]{2,1,0:T(8,128)(2,1)S(1)}, u32[]{:S(2)}, u32[]{:S(2)}) collective-permute-start(bf16[64,16,128]{2,1,0:T(8,128)(2,1)S(1)} %bitcast.41), channel_id=1, source_target_pairs={{0,1},{1,2},{2,3},{4,5},{5,6},{6,7},{8,9},{9,10},{10,11},{12,13},{... | collective-permute-start | bytes 786440 | tf_op jit(solution)/shard_map/ppermute | solution.py:219
  93.6 16.1 %collective-permute-start.10 = (bf16[64,16,128]{2,1,0:T(8,128)(2,1)S(1)}, bf16[64,16,128]{2,1,0:T(8,128)(2,1)S(1)}, u32[]{:S(2)}, u32[]{:S(2)}) collective-permute-start(bf16[64,16,128]{2,1,0:T(8,128)(2,1)S(1)} %bitcast.42), channel_id=1, source_target_pairs={{1,0},{2,1},{3,2},{5,4},{6,5},{7,6},{9,8},{10,9},{11,10},{13,12},{... | collective-permute-start | bytes 786440 | tf_op jit(solution)/shard_map/ppermute | solution.py:220
  123.9 9.6 %collective-permute-start.22 = (bf16[16,1536]{1,0:T(8,128)(2,1)S(1)}, bf16[16,1536]{1,0:T(8,128)(2,1)S(1)}, u32[]{:S(2)}, u32[]{:S(2)}) collective-permute-start(bf16[16,1536]{1,0:T(8,128)(2,1)S(1)} %get-tuple-element.44), channel_id=1, source_target_pairs={{0,3},{1,0},{2,1},{3,2},{4,7},{5,4},{6,5},{7,6},{8,11},{9,8},{10,9... | collective-permute-start | bytes 147464 | tf_op jit(solution)/shard_map/ppermute | solution.py:198
  134.6 11.3 %collective-permute-start.23 = (f32[16,1536]{1,0:T(8,128)S(1)}, f32[16,1536]{1,0:T(8,128)S(1)}, u32[]{:S(2)}, u32[]{:S(2)}) collective-permute-start(f32[16,1536]{1,0:T(8,128)S(1)} %get-tuple-element.19), channel_id=1, source_target_pairs={{0,3},{1,0},{2,1},{3,2},{4,7},{5,4},{6,5},{7,6},{8,11},{9,8},{10,9... | collective-permute-start | bytes 294920 | tf_op jit(solution)/shard_map/ppermute | solution.py:205
  137.4 11.8 %collective-permute-start.24 = (f32[16,1536]{1,0:T(8,128)S(1)}, f32[16,1536]{1,0:T(8,128)S(1)}, u32[]{:S(2)}, u32[]{:S(2)}) collective-permute-start(f32[16,1536]{1,0:T(8,128)S(1)} %get-tuple-element.19), channel_id=1, source_target_pairs={{0,2},{1,3},{2,0},{3,1},{4,6},{5,7},{6,4},{7,5},{8,10},{9,11},{10,... | collective-permute-start | bytes 294920 | tf_op jit(solution)/shard_map/ppermute | solution.py:205
  137.4 11.8 %collective-permute-start.25 = (f32[16,1536]{1,0:T(8,128)S(1)}, f32[16,1536]{1,0:T(8,128)S(1)}, u32[]{:S(2)}, u32[]{:S(2)}) collective-permute-start(f32[16,1536]{1,0:T(8,128)S(1)} %get-tuple-element.19), channel_id=1, source_target_pairs={{0,1},{1,2},{2,3},{3,0},{4,5},{5,6},{6,7},{7,4},{8,9},{9,10},{10,1... | collective-permute-start | bytes 294920 | tf_op jit(solution)/shard_map/ppermute | solution.py:205
  140.9 9.2 %collective-permute-start.17 = (f32[16,1536]{1,0:T(8,128)S(1)}, f32[16,1536]{1,0:T(8,128)S(1)}, u32[]{:S(2)}, u32[]{:S(2)}) collective-permute-start(f32[16,1536]{1,0:T(8,128)S(1)} %get-tuple-element.17), channel_id=1, source_target_pairs={{0,3},{1,0},{2,1},{3,2},{4,7},{5,4},{6,5},{7,6},{8,11},{9,8},{10,9... | collective-permute-start | bytes 294920 | tf_op jit(solution)/shard_map/ppermute | solution.py:205
  141.7 12.4 %collective-permute-start.18 = (f32[16,1536]{1,0:T(8,128)S(1)}, f32[16,1536]{1,0:T(8,128)S(1)}, u32[]{:S(2)}, u32[]{:S(2)}) collective-permute-start(f32[16,1536]{1,0:T(8,128)S(1)} %get-tuple-element.17), channel_id=1, source_target_pairs={{0,2},{1,3},{2,0},{3,1},{4,6},{5,7},{6,4},{7,5},{8,10},{9,11},{10,... | collective-permute-start | bytes 294920 | tf_op jit(solution)/shard_map/ppermute | solution.py:205
  145.9 10.1 %collective-permute-start.19 = (f32[16,1536]{1,0:T(8,128)S(1)}, f32[16,1536]{1,0:T(8,128)S(1)}, u32[]{:S(2)}, u32[]{:S(2)}) collective-permute-start(f32[16,1536]{1,0:T(8,128)S(1)} %get-tuple-element.17), channel_id=1, source_target_pairs={{0,1},{1,2},{2,3},{3,0},{4,5},{5,6},{6,7},{7,4},{8,9},{9,10},{10,1... | collective-permute-start | bytes 294920 | tf_op jit(solution)/shard_map/ppermute | solution.py:205
  (22 other events, 134.4 us)

commit v3 on v2

--- a/solution.py
+++ b/solution.py
@@ -49,13 +49,14 @@
         part_ref[c : c + 1, :] = jnp.sum(aligned, axis=0, keepdims=True)
 
 
-def conv_back(low, mid, high, feat_reversed, grad, base, earlier, start, size):
-    channels, rows, width = mid.shape
+def conv_back(low, mid, high, feat_reversed, grad, base, earlier, first, start, channels, size):
+    rows, width = mid.shape[1:]
     take = low.shape[1]
     total = base.shape[1]
     group = math.gcd(channels, GROUP)
-    skip = start // group
+    skip, near = start // group, (start - first) // group
     own = lambda *dims: pl.BlockSpec((group,) + dims, lambda i: (i,) + (0,) * len(dims))
+    rim = lambda *dims: pl.BlockSpec((group,) + dims, lambda i: (i + near,) + (0,) * len(dims))
     part = lambda *dims: pl.BlockSpec((group,) + dims, lambda i: (i + skip,) + (0,) * len(dims))
     more = [] if earlier is None else [earlier]
     return pl.pallas_call(
@@ -65,7 +66,7 @@
             jax.ShapeDtypeStruct(grad.shape, jnp.float32),
             jax.ShapeDtypeStruct((channels, total), jnp.float32),
         ),
-        in_specs=[own(take, width), own(rows, width), own(take, width)]
+        in_specs=[rim(take, width), rim(rows, width), rim(take, width)]
         + [part(rows, width), part(rows, width), part(total)]
         + [pl.BlockSpec(memory_space=pl.ANY) for _ in more],
         out_specs=(part(rows, width), own(total)),
@@ -160,24 +161,7 @@
     for step in list(range(1, chips)) + [0]:
         away = swap(part(2 * step + 1).astype(jnp.bfloat16))
         pair[step] = part(2 * step) + away.astype(jnp.float32)
-    pieces = 2 if local_ch % 32 == 0 else 1
-    chunk = local_ch // pieces
-
-    w_in_sum, w_out_sum = None, None
-    span, bit = w_in.shape[1], 1
-    while bit < hops:
-        span //= 2
-        pairs = [(i, i ^ bit) for i in range(hops)]
-        trade = lambda value: lax.ppermute(value.astype(jnp.bfloat16), "sp", pairs).astype(jnp.float32)
-        if bit == 1:
-            w_in_away = trade(contract_last(mixed_all, preact_grad[span:]))
-            w_out_away = trade(contract_last(hidden[span:], grad_all))
-            w_in_sum = contract_last(mixed_all, preact_grad[:span]) + w_in_away
-            w_out_sum = contract_last(hidden[:span], grad_all) + w_out_away
-        else:
-            w_in_sum = w_in_sum[:, :span] + trade(w_in_sum[:, span:])
-            w_out_sum = w_out_sum[:span] + trade(w_out_sum[span:])
-        bit *= 2
+    chunk = local_ch // 2
 
     take = min(rows, up(half, 16))
     depth = rows + 2 * take
@@ -190,38 +174,112 @@
     forward = [(i, i + 1) for i in range(hops - 1)]
     backward = [(i + 1, i) for i in range(hops - 1)]
 
-    def summed(lines):
+    shift = lambda step: [(i, (i + step) % hops) for i in range(hops)]
+
+    def scattered(lines):
         each = lines.shape[0] // hops
-        shift = lambda step: [(i, (i + step) % hops) for i in range(hops)]
         cut = lambda step: lax.dynamic_slice_in_dim(lines, lax.rem(mine + step, hops) * each, each, 0)
-        come = [
+        return [cut(0)] + [
             lax.ppermute(cut(step).astype(jnp.bfloat16), "sp", shift(step)) for step in range(1, hops)
         ]
-        block = cut(0)
+
+    def added(blocks):
+        return sum((value.astype(jnp.float32) for value in blocks[1:]), blocks[0])
+
+    def spread(block):
+        return [block] + [lax.ppermute(block, "sp", shift(hops - step)) for step in range(1, hops)]
+
+    def placed(blocks):
+        each, total = blocks[0].shape
+        whole = jnp.zeros((each * hops, total), jnp.float32)
+        for step, value in enumerate(blocks):
+            whole = lax.dynamic_update_slice_in_dim(whole, value, lax.rem(mine + step, hops) * each, 0)
+        return whole
+
+    tie = lambda value, *others: lax.optimization_barrier((value,) + others)[0]
+    narrow = lambda value: value.astype(jnp.bfloat16)
+    wide = lambda value: value.astype(jnp.float32)
+
+    def arrived(piece):
+        at = slice(piece * chunk, (piece + 1) * chunk)
+        come = [
+            lax.ppermute(narrow(pair[step][at]), "ch", across(step)) for step in range(1, chips)
+        ]
+        return pair[0][at], come
+
+    def mixed(mine, come):
         for value in come:
-            block = block + value.astype(jnp.float32)
-        whole = jnp.zeros_like(lines)
-        for step in range(hops):
-            value = block if step == 0 else lax.ppermute(block, "sp", shift(hops - step))
-            whole = lax.dynamic_update_slice_in_dim(
-                whole, value, lax.rem(mine + step, hops) * each, 0
-            )
-        return whole
-
-    in_grad, lines = None, []
-    for piece in range(pieces):
-        at = slice(piece * chunk, (piece + 1) * chunk)
-        mix = pair[0][at]
-        for step in range(1, chips):
-            sent = pair[step][at].astype(jnp.bfloat16)
-            mix = mix + lax.ppermute(sent, "ch", across(step)).astype(jnp.float32)
-        mix = mix.astype(jnp.bfloat16).reshape(chunk, rows, width)
-        low = lax.ppermute(mix[:, rows - take :], "sp", forward)
-        high = lax.ppermute(mix[:, :take], "sp", backward)
-        in_grad, line = conv_back(
-            low, mix, high, feat_reversed, out_grad, base, in_grad, piece * chunk, size
+            mine = mine + wide(value)
+        return narrow(mine).reshape(chunk, rows, width)
+
+    def rimmed(mix):
+        return (
+            lax.ppermute(mix[:, rows - take :], "sp", forward),
+            mix,
+            lax.ppermute(mix[:, :take], "sp", backward),
         )
-        lines.append(summed(line))
+
+    def traded(values, bit):
+        pairs = [(i, i ^ bit) for i in range(hops)]
+        return [lax.ppermute(value, "sp", pairs) for value in values]
+
+    span = w_in.shape[1] // 2
+    part_ch = chunk // 2
+
+    def conv(rim, earlier, index):
+        return conv_back(
+            *rim, feat_reversed, out_grad, base, earlier, index // 2 * chunk, index * part_ch, part_ch, size
+        )
+
+    mine_a, come_a = arrived(0)
+    mine_b, come_b = arrived(1)
+    mix_a = mixed(mine_a, come_a)
+    rim_a = rimmed(mix_a)
+    late_grad, late_hidden = lax.optimization_barrier((preact_grad, hidden, mix_a))[:2]
+    sent = (
+        narrow(contract_last(mixed_all, late_grad[span:])),
+        narrow(contract_last(late_hidden[span:], grad_all)),
+    )
+    w_in_sum = contract_last(mixed_all, late_grad[:span])
+    w_out_sum = contract_last(late_hidden[:span], grad_all)
+    away = traded(sent, 1)
+    w_in_sum, w_out_sum, low = lax.optimization_barrier((w_in_sum, w_out_sum, rim_a[0], *sent))[:3]
+    rim_a = (low,) + rim_a[1:]
+    in_grad, line0 = conv(rim_a, None, 0)
+    come_b = [tie(value, line0) for value in come_b]
+    mix_b = mixed(mine_b, come_b)
+    rim_b = rimmed(mix_b)
+    in_grad, line1 = conv((tie(rim_a[0], mix_b), rim_a[1], rim_a[2]), in_grad, 1)
+    away = [tie(value, line1) for value in away]
+    w_in_sum = w_in_sum + wide(away[0])
+    w_out_sum = w_out_sum + wide(away[1])
+    w_sums, bit, sent = (w_in_sum, w_out_sum), 2, ()
+
+    def halves(sums, span):
+        return (narrow(sums[0][:, span:]), narrow(sums[1][span:]))
+
+    if bit < hops:
+        span //= 2
+        sent = halves(w_sums, span)
+        away = traded(sent, bit)
+    blocks_a = scattered(jnp.concatenate([line0, line1], axis=0))
+    in_grad, line2 = conv((tie(rim_b[0], *sent), rim_b[1], rim_b[2]), in_grad, 2)
+    if bit < hops:
+        away = [tie(value, line2) for value in away]
+    while bit < hops:
+        w_sums = (w_sums[0][:, :span] + wide(away[0]), w_sums[1][:span] + wide(away[1]))
+        bit *= 2
+        if bit < hops:
+            span //= 2
+            away = traded(halves(w_sums, span), bit)
+    w_in_sum, w_out_sum = w_sums
+    block_a = added([blocks_a[0]] + [tie(value, line2) for value in blocks_a[1:]])
+    whole_a = spread(block_a)
+    in_grad, line3 = conv((tie(rim_b[0], block_a), rim_b[1], rim_b[2]), in_grad, 3)
+    line3 = lax.optimization_barrier((line3, *whole_a[1:]))
+    whole_a = [whole_a[0], *line3[1:]]
+    blocks_b = scattered(jnp.concatenate([line2, line3[0]], axis=0))
+    lines = [placed(whole_a), placed(spread(added(blocks_b)))]
 
     def absolute(value, dim):
         blocks = []

time: 160 us -> 149 us (0.931)
  waiting for transfers between devices: 51 us -> 41 us
  starting transfers between devices: 40.7 us -> 38.8 us
    ppermute x22, waiting for transfers between devices: 39.1 us -> 26.4 us  [the longest x2 11.7 us: arrived(): lax.ppermute(narrow(pair[step][at]), 'ch', across(step))]
    ppermute x22, starting transfers between devices: 36.6 us -> 34.7 us  [the longest x6 10.1 us: scattered(): lax.ppermute(cut(step).astype(jnp.bfloat16), 'sp', shift(step))]
    ppermute x2, waiting for transfers between devices: 11.9 us -> 13.6 us  [gathered(): lax.ppermute(block, 'ch', across(chips - step))]
    pallas_call x2 -> x4, Pallas kernels: 28.5 us -> 29.3 us  [conv_back(): pl.pallas_call(functools.partial(conv_kernel, size, take), grid=(channels...]
    unnamed x43 -> x39, local copies, waits for them, and re-layouts: 12.6 us -> 12.7 us
  transfers between devices with their start and end apart: 30 -> 30, of which waited for: 13 -> 9; matrix products, arithmetic and copies ran while one was open for 17% -> 18% of each run, Pallas kernels for 9% -> 20%
where the time goes in v3:
time: 149 us; the launch traced here: 148 us
  waiting for transfers between devices  41 us (28%)
  starting transfers between devices  38.8 us (26%)
  Pallas kernels  29.3 us (20%)
  local copies, waits for them, and re-layouts  21.8 us (15%)
  matrix products  12.3 us (8%)
  other arithmetic  3.66 us (2%)
    pallas_call x4, Pallas kernels, conv_back(): pl.pallas_call(functools.partial(conv_kernel, size, take), grid=(channels...  29.3 us
    ppermute x2, waiting for transfers between devices, gathered(): lax.ppermute(block, 'ch', across(chips - step))  13.6 us
    unnamed x39, local copies, waits for them, and re-layouts  12.7 us
    ppermute x2, waiting for transfers between devices, arrived(): lax.ppermute(narrow(pair[step][at]), 'ch', across(step))  11.7 us
    ppermute x6, starting transfers between devices, scattered(): lax.ppermute(cut(step).astype(jnp.bfloat16), 'sp', shift(step))  10.1 us
    ppermute x6, starting transfers between devices, spread(): lax.ppermute(block, 'sp', shift(hops - step))  8.56 us
    dot_general x5, matrix products, matmul(): return jnp.dot(left, right, preferred_element_type=jnp.float32)  5.86 us
    ppermute x4, starting transfers between devices, traded(): return [lax.ppermute(value, 'sp', pairs) for value in values]  5.7 us
  transfers between devices with their start and end apart: 30, of which 9 were waited for; matrix products, arithmetic and copies ran while one was open for 18% of the time, Pallas kernels for 20%

profile of v3, /device:TPU:0, one launch (start us, length us, event | category | flops | bytes accessed | tf_op | source)
XLA Modules:
  0.0 148.3 jit_solution(15112084290843164794)
XLA Ops:
  0.7 2.1 %copy.31 = bf16[16,8,16,128]{3,1,2,0:T(8,128)(2,1)} copy(bf16[16,8,16,128]{3,2,1,0:T(8,128)(2,1)} %bitcast.46) | data formatting | bytes 1048576
  3.2 2.5 %collective-permute-start.4 = (bf16[128,2048]{1,0:T(8,128)(2,1)}, bf16[128,2048]{1,0:T(8,128)(2,1)}, u32[]{:S(2)}, u32[]{:S(2)}) collective-permute-start(bf16[128,2048]{1,0:T(8,128)(2,1)} %bitcast.32), channel_id=1, source_target_pairs={{0,8},{4,12},{8,0},{12,4},{1,9},{5,13},{9,1},{13,5},{2,10},{6,14},... | collective-permute-start | bytes 1572872 | tf_op jit(solution)/shard_map/ppermute | solution.py:131
  5.7 2.0 %copy.32 = bf16[16,8,16,128]{3,1,2,0:T(8,128)(2,1)} copy(bf16[16,8,16,128]{3,2,1,0:T(8,128)(2,1)} %bitcast.36) | data formatting | bytes 1048576
  12.3 6.5 %collective-permute-done.4 = bf16[128,2048]{1,0:T(8,128)(2,1)} collective-permute-done((bf16[128,2048]{1,0:T(8,128)(2,1)}, bf16[128,2048]{1,0:T(8,128)(2,1)}, u32[]{:S(2)}, u32[]{:S(2)}) %collective-permute-start.4) | collective-permute-done | bytes 524320 | tf_op jit(solution)/shard_map/ppermute | solution.py:131
  20.7 1.9 %constant_dynamic-update-slice_fusion.5 = bf16[512,2048]{1,0:T(8,128)(2,1)} fusion(bf16[512,2048]{1,0:T(8,128)(2,1)} %constant_dynamic-update-slice_fusion.6, bf16[128,2048]{1,0:T(8,128)(2,1)} %collective-permute-done.4), kind=kLoop, calls=%fused_computation.70 | loop fusion | bytes 1048576
  22.6 7.2 %collective-permute-done.1 = bf16[128,2048]{1,0:T(8,128)(2,1)S(1)} collective-permute-done((bf16[128,2048]{1,0:T(8,128)(2,1)}, bf16[128,2048]{1,0:T(8,128)(2,1)S(1)}, u32[]{:S(2)}, u32[]{:S(2)}) %collective-permute-start.1) | collective-permute-done | bytes 524320 | tf_op jit(solution)/shard_map/ppermute | solution.py:131
  33.4 3.4 %multiply_convert_fusion = (bf16[512,2048]{1,0:T(8,128)(2,1)S(1)}, f32[512,2048]{1,0:T(8,128)S(1)}) fusion(bf16[512,2048]{1,0:T(8,128)(2,1)} %constant_dynamic-update-slice_fusion.4, bf16[512,128]{1,0:T(8,128)(2,1)S(1)} %get-tuple-element.79, bf16[512,128]{1,0:T(8,128)(2,1)S(1)} %get-tuple-element.80, bf16[512,128]{1,0:T(8,128)(2,1)S(1)} %copy-done.6, ...), kind=kOutput, calls=%fused_computation.7 | convolution fusion | flops 1081081856 | bytes 8912896 | tf_op jit(solution)/shard_map/dot_general | solution.py:90
  36.9 4.1 %fusion.5 = bf16[512,2048]{1,0:T(8,128)(2,1)S(1)} fusion(f32[512,2048]{1,0:T(8,128)S(1)} %get-tuple-element.101, bf16[512,2048]{1,0:T(8,128)(2,1)S(1)} %constant_dynamic-update-slice_fusion, bf16[128,512]{1,0:T(8,128)(2,1)S(1)} %copy-done.10, bf16[128,512]{1,0:T(8,128)(2,1)S(1)} %copy-done.11, bf16[128,512]{1,0:T(8,128)(2,1)S(1)} %copy-done.12, ...), kind=kOutput, calls=%fused_computation.6 | convolution fusion | flops 1086324736 | bytes 8912896 | tf_op jit(solution)/shard_map/dot_general | solution.py:96
  46.6 11.7 %collective-permute-done.9 = bf16[64,2048]{1,0:T(8,128)(2,1)S(1)} collective-permute-done((bf16[64,2048]{1,0:T(8,128)(2,1)S(1)}, bf16[64,2048]{1,0:T(8,128)(2,1)S(1)}, u32[]{:S(2)}, u32[]{:S(2)}) %collective-permute-start.9) | collective-permute-done | bytes 262176 | tf_op jit(solution)/shard_map/ppermute | solution.py:206
  58.4 3.7 %collective-permute-start.10 = (bf16[64,16,128]{2,1,0:T(8,128)(2,1)S(1)}, bf16[64,16,128]{2,1,0:T(8,128)(2,1)S(1)}, u32[]{:S(2)}, u32[]{:S(2)}) collective-permute-start(bf16[64,16,128]{2,1,0:T(8,128)(2,1)S(1)} %bitcast.42), channel_id=1, source_target_pairs={{0,1},{1,2},{2,3},{4,5},{5,6},{6,7},{8,9},{9,10},{10,11},{12,13},{... | collective-permute-start | bytes 786440 | tf_op jit(solution)/shard_map/ppermute | solution.py:217
  65.9 2.7 %collective-permute-start.14 = (bf16[512,256]{1,0:T(8,128)(2,1)S(1)}, bf16[512,256]{1,0:T(8,128)(2,1)S(1)}, u32[]{:S(2)}, u32[]{:S(2)}) collective-permute-start(bf16[512,256]{1,0:T(8,128)(2,1)S(1)} %convolution_convert_fusion.3), channel_id=1, source_target_pairs={{0,1},{1,0},{2,3},{3,2},{4,5},{5,4},{6,7},{7,6},{8,9},{9,8},{10,11... | collective-permute-start | bytes 786440 | tf_op jit(solution)/shard_map/ppermute | solution.py:224
  69.5 5.4 %collective-permute-done.11.high_ref = bf16[64,16,128]{2,1,0:T(8,128)(2,1)S(1)} collective-permute-done((bf16[64,16,128]{2,1,0:T(8,128)(2,1)S(1)}, bf16[64,16,128]{2,1,0:T(8,128)(2,1)S(1)}, u32[]{:S(2)}, u32[]{:S(2)}) %collective-permute-start.11) | collective-permute-done | bytes 262176 | tf_op jit(solution)/shard_map/ppermute | solution.py:219
  74.8 7.3 %shard_map.93 = (f32[128,16,128]{2,1,0:T(8,128)}, f32[32,1536]{1,0:T(8,128)S(1)}) custom-call(bf16[64,16,128]{2,1,0:T(8,128)(2,1)S(1)} %collective-permute-done.10.low_ref, bf16[64,16,128]{2,1,0:T(8,128)(2,1)S(1)} %bitcast.44, bf16[64,16,128]{2,1,0:T(8,128)(2,1)S(1)} %collective-permute-done.11.high_ref, bf16[128,16,128]{2,1,0:T(8,128)(2,1)S(1)} %rev.12.feat_ref, ...), custom_call_target="tpu_custom_call" | custom-call | flops 3221225472 | bytes 1310720 | tf_op jit(solution)/shard_map/pallas_call | solution.py:62
  85.3 7.4 %shard_map.94 = (f32[128,16,128]{2,1,0:T(8,128)}, f32[32,1536]{1,0:T(8,128)S(1)}) custom-call(bf16[64,16,128]{2,1,0:T(8,128)(2,1)S(1)} %collective-permute-done.10.low_ref, bf16[64,16,128]{2,1,0:T(8,128)(2,1)S(1)} %bitcast.45, bf16[64,16,128]{2,1,0:T(8,128)(2,1)S(1)} %collective-permute-done.11.high_ref, ...), custom_call_target="tpu_custom_call", output_to_operand_aliasing={{0}: (6, {})} | custom-call | flops 3221225472 | bytes 1310720 | tf_op jit(solution)/shard_map/pallas_call | solution.py:62
  92.7 4.9 %collective-permute-start.18 = (bf16[16,1536]{1,0:T(8,128)(2,1)S(1)}, bf16[16,1536]{1,0:T(8,128)(2,1)S(1)}, u32[]{:S(2)}, u32[]{:S(2)}) collective-permute-start(bf16[16,1536]{1,0:T(8,128)(2,1)S(1)} %get-tuple-element.90), channel_id=1, source_target_pairs={{0,3},{1,0},{2,1},{3,2},{4,7},{5,4},{6,5},{7,6},{8,11},{9,8},{10,9... | collective-permute-start | bytes 147464 | tf_op jit(solution)/shard_map/ppermute | solution.py:183
  98.5 2.4 %collective-permute-start.29 = (bf16[128,512]{1,0:T(8,128)(2,1)S(1)}, bf16[128,512]{1,0:T(8,128)(2,1)S(1)}, u32[]{:S(2)}, u32[]{:S(2)}) collective-permute-start(bf16[128,512]{1,0:T(8,128)(2,1)S(1)} %slice.136), channel_id=1, source_target_pairs={{0,2},{1,3},{2,0},{3,1},{4,6},{5,7},{6,4},{7,5},{8,10},{9,11},{10,... | collective-permute-start | bytes 393224 | tf_op jit(solution)/shard_map/ppermute | solution.py:224
  101.4 2.0 %collective-permute-start.13 = (bf16[16,1536]{1,0:T(8,128)(2,1)S(1)}, bf16[16,1536]{1,0:T(8,128)(2,1)S(1)}, u32[]{:S(2)}, u32[]{:S(2)}) collective-permute-start(bf16[16,1536]{1,0:T(8,128)(2,1)S(1)} %get-tuple-element.89), channel_id=1, source_target_pairs={{0,1},{1,2},{2,3},{3,0},{4,5},{5,6},{6,7},{7,4},{8,9},{9,10},{10,1... | collective-permute-start | bytes 147464 | tf_op jit(solution)/shard_map/ppermute | solution.py:183
  103.4 7.3 %shard_map.95 = (f32[128,16,128]{2,1,0:T(8,128)}, f32[32,1536]{1,0:T(8,128)S(1)}) custom-call(bf16[64,16,128]{2,1,0:T(8,128)(2,1)S(1)} %collective-permute-done.12.low_ref, bf16[64,16,128]{2,1,0:T(8,128)(2,1)S(1)} %bitcast.40, bf16[64,16,128]{2,1,0:T(8,128)(2,1)S(1)} %collective-permute-done.16.high_ref, ...), custom_call_target="tpu_custom_call", output_to_operand_aliasing={{0}: (6, {})} | custom-call | flops 3221225472 | bytes 1310720 | tf_op jit(solution)/shard_map/pallas_call | solution.py:62
  114.3 1.9 %collective-permute-start.21 = (f32[16,1536]{1,0:T(8,128)S(1)}, f32[16,1536]{1,0:T(8,128)S(1)}, u32[]{:S(2)}, u32[]{:S(2)}) collective-permute-start(f32[16,1536]{1,0:T(8,128)S(1)} %get-tuple-element.65), channel_id=1, source_target_pairs={{0,1},{1,2},{2,3},{3,0},{4,5},{5,6},{6,7},{7,4},{8,9},{9,10},{10,1... | collective-permute-start | bytes 294920 | tf_op jit(solution)/shard_map/ppermute | solution.py:190
  117.2 7.3 %shard_map.96 = (f32[128,16,128]{2,1,0:T(8,128)}, f32[32,1536]{1,0:T(8,128)S(1)}) custom-call(bf16[64,16,128]{2,1,0:T(8,128)(2,1)S(1)} %collective-permute-done.12.low_ref, bf16[64,16,128]{2,1,0:T(8,128)(2,1)S(1)} %bitcast.41, bf16[64,16,128]{2,1,0:T(8,128)(2,1)S(1)} %collective-permute-done.16.high_ref, ...), custom_call_target="tpu_custom_call", output_to_operand_aliasing={{0}: (6, {})} | custom-call | flops 3221225472 | bytes 1310720 | tf_op jit(solution)/shard_map/pallas_call | solution.py:62
  125.3 1.9 %collective-permute-start.24 = (bf16[16,1536]{1,0:T(8,128)(2,1)S(1)}, bf16[16,1536]{1,0:T(8,128)(2,1)S(1)}, u32[]{:S(2)}, u32[]{:S(2)}) collective-permute-start(bf16[16,1536]{1,0:T(8,128)(2,1)S(1)} %get-tuple-element.87), channel_id=1, source_target_pairs={{0,3},{1,0},{2,1},{3,2},{4,7},{5,4},{6,5},{7,6},{8,11},{9,8},{10,9... | collective-permute-start | bytes 147464 | tf_op jit(solution)/shard_map/ppermute | solution.py:183
  130.0 2.6 %collective-permute-done.23 = bf16[16,1536]{1,0:T(8,128)(2,1)S(1)} collective-permute-done((bf16[16,1536]{1,0:T(8,128)(2,1)S(1)}, bf16[16,1536]{1,0:T(8,128)(2,1)S(1)}, u32[]{:S(2)}, u32[]{:S(2)}) %collective-permute-start.23) | collective-permute-done | bytes 49184 | tf_op jit(solution)/shard_map/ppermute | solution.py:183
  137.2 2.0 %collective-permute-start.27 = (f32[16,1536]{1,0:T(8,128)}, f32[16,1536]{1,0:T(8,128)S(1)}, u32[]{:S(2)}, u32[]{:S(2)}) collective-permute-start(f32[16,1536]{1,0:T(8,128)} %get-tuple-element.67), channel_id=1, source_target_pairs={{0,1},{1,2},{2,3},{3,0},{4,5},{5,6},{6,7},{7,4},{8,9},{9,10},{10,1... | collective-permute-start | bytes 294920 | tf_op jit(solution)/shard_map/ppermute | solution.py:190
  140.1 4.5 %collective-permute-done.26 = f32[16,1536]{1,0:T(8,128)S(1)} collective-permute-done((f32[16,1536]{1,0:T(8,128)}, f32[16,1536]{1,0:T(8,128)S(1)}, u32[]{:S(2)}, u32[]{:S(2)}) %collective-permute-start.26) | collective-permute-done | bytes 98336 | tf_op jit(solution)/shard_map/ppermute | solution.py:190
  (138 shorter events, 42.2 us)
Async XLA Ops:
  2.7 16.1 %collective-permute-start.3 = (bf16[128,2048]{1,0:T(8,128)(2,1)}, bf16[128,2048]{1,0:T(8,128)(2,1)}, u32[]{:S(2)}, u32[]{:S(2)}) collective-permute-start(bf16[128,2048]{1,0:T(8,128)(2,1)} %bitcast.32), channel_id=1, source_target_pairs={{0,4},{4,0},{8,12},{12,8},{1,5},{5,1},{9,13},{13,9},{2,6},{6,2},{1... | collective-permute-start | bytes 1572872 | tf_op jit(solution)/shard_map/ppermute | solution.py:121
  3.2 15.6 %collective-permute-start.4 = (bf16[128,2048]{1,0:T(8,128)(2,1)}, bf16[128,2048]{1,0:T(8,128)(2,1)}, u32[]{:S(2)}, u32[]{:S(2)}) collective-permute-start(bf16[128,2048]{1,0:T(8,128)(2,1)} %bitcast.32), channel_id=1, source_target_pairs={{0,8},{4,12},{8,0},{12,4},{1,9},{5,13},{9,1},{13,5},{2,10},{6,14},... | collective-permute-start | bytes 1572872 | tf_op jit(solution)/shard_map/ppermute | solution.py:131
  7.7 22.1 %collective-permute-start = (bf16[128,2048]{1,0:T(8,128)(2,1)}, bf16[128,2048]{1,0:T(8,128)(2,1)}, u32[]{:S(2)}, u32[]{:S(2)}) collective-permute-start(bf16[128,2048]{1,0:T(8,128)(2,1)} %bitcast.33), channel_id=1, source_target_pairs={{0,4},{4,0},{8,12},{12,8},{1,5},{5,1},{9,13},{13,9},{2,6},{6,2},{1... | collective-permute-start | bytes 1572872 | tf_op jit(solution)/shard_map/ppermute | solution.py:121
  7.9 21.8 %collective-permute-start.1 = (bf16[128,2048]{1,0:T(8,128)(2,1)}, bf16[128,2048]{1,0:T(8,128)(2,1)S(1)}, u32[]{:S(2)}, u32[]{:S(2)}) collective-permute-start(bf16[128,2048]{1,0:T(8,128)(2,1)} %bitcast.33), channel_id=1, source_target_pairs={{0,8},{4,12},{8,0},{12,4},{1,9},{5,13},{9,1},{13,5},{2,10},{6,14},... | collective-permute-start | bytes 1572872 | tf_op jit(solution)/shard_map/ppermute | solution.py:131
  18.8 13.7 %collective-permute-start.5 = (bf16[128,2048]{1,0:T(8,128)(2,1)}, bf16[128,2048]{1,0:T(8,128)(2,1)S(1)}, u32[]{:S(2)}, u32[]{:S(2)}) collective-permute-start(bf16[128,2048]{1,0:T(8,128)(2,1)} %collective-permute-done.4), channel_id=1, source_target_pairs={{0,4},{4,0},{8,12},{12,8},{1,5},{5,1},{9,13},{13,9},{2,6},{6,2},{1... | collective-permute-start | bytes 1572872 | tf_op jit(solution)/shard_map/ppermute | solution.py:121
  29.8 7.1 %collective-permute-start.2 = (bf16[128,2048]{1,0:T(8,128)(2,1)S(1)}, bf16[128,2048]{1,0:T(8,128)(2,1)S(1)}, u32[]{:S(2)}, u32[]{:S(2)}) collective-permute-start(bf16[128,2048]{1,0:T(8,128)(2,1)S(1)} %collective-permute-done.1), channel_id=1, source_target_pairs={{0,4},{4,0},{8,12},{12,8},{1,5},{5,1},{9,13},{13,9},{2,6},{6,2},{1... | collective-permute-start | bytes 1572872 | tf_op jit(solution)/shard_map/ppermute | solution.py:121
  44.1 38.1 %collective-permute-start.8 = (bf16[64,2048]{1,0:T(8,128)(2,1)S(1)}, bf16[64,2048]{1,0:T(8,128)(2,1)S(1)}, u32[]{:S(2)}, u32[]{:S(2)}) collective-permute-start(bf16[64,2048]{1,0:T(8,128)(2,1)S(1)} %get-tuple-element.69), channel_id=1, source_target_pairs={{0,8},{4,12},{8,0},{12,4},{1,9},{5,13},{9,1},{13,5},{2,10},{6,14},... | collective-permute-start | bytes 786440 | tf_op jit(solution)/shard_map/ppermute | solution.py:206
  45.9 12.4 %collective-permute-start.9 = (bf16[64,2048]{1,0:T(8,128)(2,1)S(1)}, bf16[64,2048]{1,0:T(8,128)(2,1)S(1)}, u32[]{:S(2)}, u32[]{:S(2)}) collective-permute-start(bf16[64,2048]{1,0:T(8,128)(2,1)S(1)} %get-tuple-element.68), channel_id=1, source_target_pairs={{0,8},{4,12},{8,0},{12,4},{1,9},{5,13},{9,1},{13,5},{2,10},{6,14},... | collective-permute-start | bytes 786440 | tf_op jit(solution)/shard_map/ppermute | solution.py:206
  58.4 11.0 %collective-permute-start.10 = (bf16[64,16,128]{2,1,0:T(8,128)(2,1)S(1)}, bf16[64,16,128]{2,1,0:T(8,128)(2,1)S(1)}, u32[]{:S(2)}, u32[]{:S(2)}) collective-permute-start(bf16[64,16,128]{2,1,0:T(8,128)(2,1)S(1)} %bitcast.42), channel_id=1, source_target_pairs={{0,1},{1,2},{2,3},{4,5},{5,6},{6,7},{8,9},{9,10},{10,11},{12,13},{... | collective-permute-start | bytes 786440 | tf_op jit(solution)/shard_map/ppermute | solution.py:217
  63.7 11.1 %collective-permute-start.11 = (bf16[64,16,128]{2,1,0:T(8,128)(2,1)S(1)}, bf16[64,16,128]{2,1,0:T(8,128)(2,1)S(1)}, u32[]{:S(2)}, u32[]{:S(2)}) collective-permute-start(bf16[64,16,128]{2,1,0:T(8,128)(2,1)S(1)} %bitcast.43), channel_id=1, source_target_pairs={{1,0},{2,1},{3,2},{5,4},{6,5},{7,6},{9,8},{10,9},{11,10},{13,12},{... | collective-permute-start | bytes 786440 | tf_op jit(solution)/shard_map/ppermute | solution.py:219
  65.9 31.7 %collective-permute-start.14 = (bf16[512,256]{1,0:T(8,128)(2,1)S(1)}, bf16[512,256]{1,0:T(8,128)(2,1)S(1)}, u32[]{:S(2)}, u32[]{:S(2)}) collective-permute-start(bf16[512,256]{1,0:T(8,128)(2,1)S(1)} %convolution_convert_fusion.3), channel_id=1, source_target_pairs={{0,1},{1,0},{2,3},{3,2},{4,5},{5,4},{6,7},{7,6},{8,9},{9,8},{10,11... | collective-permute-start | bytes 786440 | tf_op jit(solution)/shard_map/ppermute | solution.py:224
  68.6 29.1 %collective-permute-start.15 = (bf16[256,512]{1,0:T(8,128)(2,1)S(1)}, bf16[256,512]{1,0:T(8,128)(2,1)S(1)}, u32[]{:S(2)}, u32[]{:S(2)}) collective-permute-start(bf16[256,512]{1,0:T(8,128)(2,1)S(1)} %convolution_convert_fusion.2), channel_id=1, source_target_pairs={{0,1},{1,0},{2,3},{3,2},{4,5},{5,4},{6,7},{7,6},{8,9},{9,8},{10,11... | collective-permute-start | bytes 786440 | tf_op jit(solution)/shard_map/ppermute | solution.py:224
  82.3 18.6 %collective-permute-start.12 = (bf16[64,16,128]{2,1,0:T(8,128)(2,1)S(1)}, bf16[64,16,128]{2,1,0:T(8,128)(2,1)S(1)}, u32[]{:S(2)}, u32[]{:S(2)}) collective-permute-start(bf16[64,16,128]{2,1,0:T(8,128)(2,1)S(1)} %bitcast.38), channel_id=1, source_target_pairs={{0,1},{1,2},{2,3},{4,5},{5,6},{6,7},{8,9},{9,10},{10,11},{12,13},{... | collective-permute-start | bytes 786440 | tf_op jit(solution)/shard_map/ppermute | solution.py:217
  84.0 17.4 %collective-permute-start.16 = (bf16[64,16,128]{2,1,0:T(8,128)(2,1)S(1)}, bf16[64,16,128]{2,1,0:T(8,128)(2,1)S(1)}, u32[]{:S(2)}, u32[]{:S(2)}) collective-permute-start(bf16[64,16,128]{2,1,0:T(8,128)(2,1)S(1)} %bitcast.39), channel_id=1, source_target_pairs={{1,0},{2,1},{3,2},{5,4},{6,5},{7,6},{9,8},{10,9},{11,10},{13,12},{... | collective-permute-start | bytes 786440 | tf_op jit(solution)/shard_map/ppermute | solution.py:219
  92.7 18.0 %collective-permute-start.18 = (bf16[16,1536]{1,0:T(8,128)(2,1)S(1)}, bf16[16,1536]{1,0:T(8,128)(2,1)S(1)}, u32[]{:S(2)}, u32[]{:S(2)}) collective-permute-start(bf16[16,1536]{1,0:T(8,128)(2,1)S(1)} %get-tuple-element.90), channel_id=1, source_target_pairs={{0,3},{1,0},{2,1},{3,2},{4,7},{5,4},{6,5},{7,6},{8,11},{9,8},{10,9... | collective-permute-start | bytes 147464 | tf_op jit(solution)/shard_map/ppermute | solution.py:183
  97.9 12.9 %collective-permute-start.17 = (bf16[16,1536]{1,0:T(8,128)(2,1)S(1)}, bf16[16,1536]{1,0:T(8,128)(2,1)S(1)}, u32[]{:S(2)}, u32[]{:S(2)}) collective-permute-start(bf16[16,1536]{1,0:T(8,128)(2,1)S(1)} %get-tuple-element.91), channel_id=1, source_target_pairs={{0,2},{1,3},{2,0},{3,1},{4,6},{5,7},{6,4},{7,5},{8,10},{9,11},{10,... | collective-permute-start | bytes 147464 | tf_op jit(solution)/shard_map/ppermute | solution.py:183
  98.5 17.8 %collective-permute-start.29 = (bf16[128,512]{1,0:T(8,128)(2,1)S(1)}, bf16[128,512]{1,0:T(8,128)(2,1)S(1)}, u32[]{:S(2)}, u32[]{:S(2)}) collective-permute-start(bf16[128,512]{1,0:T(8,128)(2,1)S(1)} %slice.136), channel_id=1, source_target_pairs={{0,2},{1,3},{2,0},{3,1},{4,6},{5,7},{6,4},{7,5},{8,10},{9,11},{10,... | collective-permute-start | bytes 393224 | tf_op jit(solution)/shard_map/ppermute | solution.py:224
  100.9 15.5 %collective-permute-start.28 = (bf16[512,128]{1,0:T(8,128)(2,1)S(1)}, bf16[512,128]{1,0:T(8,128)(2,1)S(1)}, u32[]{:S(2)}, u32[]{:S(2)}) collective-permute-start(bf16[512,128]{1,0:T(8,128)(2,1)S(1)} %slice.137), channel_id=1, source_target_pairs={{0,2},{1,3},{2,0},{3,1},{4,6},{5,7},{6,4},{7,5},{8,10},{9,11},{10,... | collective-permute-start | bytes 393224 | tf_op jit(solution)/shard_map/ppermute | solution.py:224
  101.4 9.3 %collective-permute-start.13 = (bf16[16,1536]{1,0:T(8,128)(2,1)S(1)}, bf16[16,1536]{1,0:T(8,128)(2,1)S(1)}, u32[]{:S(2)}, u32[]{:S(2)}) collective-permute-start(bf16[16,1536]{1,0:T(8,128)(2,1)S(1)} %get-tuple-element.89), channel_id=1, source_target_pairs={{0,1},{1,2},{2,3},{3,0},{4,5},{5,6},{6,7},{7,4},{8,9},{9,10},{10,1... | collective-permute-start | bytes 147464 | tf_op jit(solution)/shard_map/ppermute | solution.py:183
  110.8 14.4 %collective-permute-start.19 = (f32[16,1536]{1,0:T(8,128)S(1)}, f32[16,1536]{1,0:T(8,128)S(1)}, u32[]{:S(2)}, u32[]{:S(2)}) collective-permute-start(f32[16,1536]{1,0:T(8,128)S(1)} %get-tuple-element.65), channel_id=1, source_target_pairs={{0,3},{1,0},{2,1},{3,2},{4,7},{5,4},{6,5},{7,6},{8,11},{9,8},{10,9... | collective-permute-start | bytes 294920 | tf_op jit(solution)/shard_map/ppermute | solution.py:190
  112.7 12.5 %collective-permute-start.20 = (f32[16,1536]{1,0:T(8,128)S(1)}, f32[16,1536]{1,0:T(8,128)S(1)}, u32[]{:S(2)}, u32[]{:S(2)}) collective-permute-start(f32[16,1536]{1,0:T(8,128)S(1)} %get-tuple-element.65), channel_id=1, source_target_pairs={{0,2},{1,3},{2,0},{3,1},{4,6},{5,7},{6,4},{7,5},{8,10},{9,11},{10,... | collective-permute-start | bytes 294920 | tf_op jit(solution)/shard_map/ppermute | solution.py:190
  114.3 10.9 %collective-permute-start.21 = (f32[16,1536]{1,0:T(8,128)S(1)}, f32[16,1536]{1,0:T(8,128)S(1)}, u32[]{:S(2)}, u32[]{:S(2)}) collective-permute-start(f32[16,1536]{1,0:T(8,128)S(1)} %get-tuple-element.65), channel_id=1, source_target_pairs={{0,1},{1,2},{2,3},{3,0},{4,5},{5,6},{6,7},{7,4},{8,9},{9,10},{10,1... | collective-permute-start | bytes 294920 | tf_op jit(solution)/shard_map/ppermute | solution.py:190
  136.7 7.9 %collective-permute-start.26 = (f32[16,1536]{1,0:T(8,128)}, f32[16,1536]{1,0:T(8,128)S(1)}, u32[]{:S(2)}, u32[]{:S(2)}) collective-permute-start(f32[16,1536]{1,0:T(8,128)} %get-tuple-element.67), channel_id=1, source_target_pairs={{0,2},{1,3},{2,0},{3,1},{4,6},{5,7},{6,4},{7,5},{8,10},{9,11},{10,... | collective-permute-start | bytes 294920 | tf_op jit(solution)/shard_map/ppermute | solution.py:190
  137.2 7.4 %collective-permute-start.27 = (f32[16,1536]{1,0:T(8,128)}, f32[16,1536]{1,0:T(8,128)S(1)}, u32[]{:S(2)}, u32[]{:S(2)}) collective-permute-start(f32[16,1536]{1,0:T(8,128)} %get-tuple-element.67), channel_id=1, source_target_pairs={{0,1},{1,2},{2,3},{3,0},{4,5},{5,6},{6,7},{7,4},{8,9},{9,10},{10,1... | collective-permute-start | bytes 294920 | tf_op jit(solution)/shard_map/ppermute | solution.py:190
  (19 other events, 101.8 us)
